TPU v7x, 256 devices: a whole 4x4x8 slice. The times are simulated.
256 devices in a mesh: grp: 8 (over y_lo, x), tp: 32 (over y_hi, z, core).
Axes of the slice: x: 4, y: 4 (y_hi: 2, y_lo: 2; y = y_hi * 2 + y_lo), z: 8, core: 2. Of those that a mesh axis runs over, the one named last changes fastest.
Arguments:
- prompt_q: bfloat16 [16384, 4096], P(('grp', 'tp')), may hold values from -8 to 8
- prompt_k: bfloat16 [16384, 1024], P(('grp', 'tp')), may hold values from -150 to 150
- prompt_v: bfloat16 [16384, 1024], P(('grp', 'tp')), may hold values from -6 to 6
- lengths: int32 [8], P('grp'), may hold values from 8192 to 16384, as said below
- sample_states: bfloat16 [128, 2, 5120], P('grp'), may hold values from -6 to 6
- norm_gain: bfloat16 [5120], replicated, may hold values from 0.099609375 to 1.8984375
- w_query: bfloat16 [5120, 4096], P(None, 'tp'), may hold values from -0.15625 to 0.15625
- b_query: bfloat16 [4096], P('tp'), may hold values from -3 to 3
- w_key: bfloat16 [5120, 1024], P(None, 'tp'), may hold values from -0.625 to 0.625
- b_key: bfloat16 [1024], P('tp'), may hold values from -3 to 3
- w_value: bfloat16 [5120, 1024], P(None, 'tp'), may hold values from -0.078125 to 0.078125
- b_value: bfloat16 [1024], P('tp'), may hold values from -3 to 3
- w_out: bfloat16 [4096, 5120], P('tp'), may hold values from -0.09375 to 0.09375
Outputs:
- prefill_mixed: bfloat16 [16384, 4096], P(('grp', 'tp'))
- decode_out: bfloat16 [128, 2, 5120], P('grp')
Inputs may be any that keep to these rules, and one draw needn't show every extreme that they name: `lengths`: one group's length is 16384 in every draw.
All inputs are finite; a program needn't handle non-finite values.
Results may differ from a plain program's by a relative error of at most 0.014.
The roundings to bfloat16 on the way count: a program that leaves them out, or rounds other values in their place, can miss the bound.
Values may be sent and summed in bfloat16 or wider, within the bound.
A program may use at most 128 MiB of HBM per device.

v0:
```python
import math

import jax
import jax.numpy as jnp
from jax import lax
from jax.sharding import PartitionSpec as P

HEADS = 32
KV_HEADS = 8
HEAD_DIM = 128


epsilon = 1e-06
rope_base = 1000000.0


def partner(value, axis, stride):
    return lax.ppermute(value, axis, [(i, i ^ 1 << stride) for i in range(lax.axis_size(axis))])


def rotate(tensor, position):
    half_dim = HEAD_DIM // 2
    frequency = rope_base ** (-(2.0 * jnp.arange(half_dim, dtype=jnp.float32)) / HEAD_DIM)
    angles = position[..., None] * frequency
    cosine_table = jnp.cos(angles)
    sine_table = jnp.sin(angles)
    front_part = tensor[..., :half_dim]
    back_part = tensor[..., half_dim:]
    return jnp.concatenate(
        [
            front_part * cosine_table - back_part * sine_table,
            back_part * cosine_table + front_part * sine_table,
        ],
        axis=-1,
    )


def joined(mine, theirs, upper):
    return jnp.where(
        upper, jnp.concatenate([theirs, mine], axis=-1), jnp.concatenate([mine, theirs], axis=-1)
    )


def absorb(carried, scores, allowed, values, pattern):
    row_max, row_sum, row_acc = carried
    masked = jnp.where(allowed, scores, -jnp.inf)
    new_max = jnp.maximum(row_max, jnp.max(masked, axis=-1))
    anchor = jnp.where(new_max == -jnp.inf, 0.0, new_max)
    weights = jnp.where(allowed, jnp.exp(scores - anchor[..., None]), 0.0)
    shrink = jnp.exp(row_max - anchor)
    row_sum = row_sum * shrink + jnp.sum(weights, axis=-1)
    gained = jnp.einsum(
        pattern, weights.astype(jnp.bfloat16), values, preferred_element_type=jnp.float32
    )
    return (new_max, row_sum, row_acc * shrink[..., None] + gained)


def prefill_sweep(carried, queries, first_query, key_rows, value_rows, first_key):
    block_width = queries.shape[1]
    key_blocks = key_rows.shape[0] // block_width
    scaling = HEAD_DIM ** (-0.5)

    def one_block(operands):
        block_no, query_block, row_max, row_sum, row_acc = operands
        query_start = first_query + block_no * block_width
        key_limit = jnp.clip((query_start + block_width - first_key) // block_width, 0, key_blocks)

        def visit_block(key_no, running):
            key_block = lax.dynamic_slice_in_dim(key_rows, key_no * block_width, block_width, 0)
            value_block = lax.dynamic_slice_in_dim(value_rows, key_no * block_width, block_width, 0)
            scores = (
                jnp.einsum(
                    "qhd,khd->hqk", query_block, key_block, preferred_element_type=jnp.float32
                )
                * scaling
            )
            query_pos = query_start + jnp.arange(block_width, dtype=jnp.int32)
            key_pos = first_key + key_no * block_width + jnp.arange(block_width, dtype=jnp.int32)
            allowed = (key_pos[None, :] <= query_pos[:, None])[None]
            return absorb(running, scores, allowed, value_block, "hqk,khd->hqd")

        return lax.fori_loop(0, key_limit, visit_block, (row_max, row_sum, row_acc))

    block_ids = jnp.arange(queries.shape[0], dtype=jnp.int32)
    return lax.map(one_block, (block_ids, queries, carried[0], carried[1], carried[2]))


def decode_sweep(carried, step_query, key_rows, value_rows, length_limit):
    scaling = HEAD_DIM ** (-0.5)
    scores = (
        jnp.einsum("rhd,khd->hrk", step_query, key_rows, preferred_element_type=jnp.float32)
        * scaling
    )
    key_pos = jnp.arange(key_rows.shape[0], dtype=jnp.int32)
    allowed = (key_pos < length_limit)[None, None, :]
    return absorb(carried, scores, allowed, value_rows, "hrk,khd->hrd")


def shards(
    prompt_q,
    prompt_k,
    prompt_v,
    lengths,
    sample_states,
    norm_gain,
    w_query,
    b_query,
    w_key,
    b_key,
    w_value,
    b_value,
    w_out,
):
    tp_count = lax.axis_size("tp")
    group_no = lax.axis_index("grp")
    tp_no = lax.axis_index("tp")
    local_heads = HEADS // tp_count
    group_size = HEADS // KV_HEADS
    prompt_rows = prompt_q.shape[0]
    block_rows = prompt_rows * tp_count
    block_width = math.gcd(block_rows, 512)
    block_count = block_rows // block_width
    scaling = HEAD_DIM ** (-0.5)
    sharing = tp_count // KV_HEADS
    levels = sharing.bit_length() - 1
    samples, step_count, model_width = sample_states.shape
    states = sample_states.astype(jnp.float32)
    normed = (
        states
        * lax.rsqrt(jnp.mean(states * states, axis=-1, keepdims=True) + epsilon)
        * norm_gain.astype(jnp.float32)
    ).astype(jnp.bfloat16)
    flat_rows = normed.reshape(samples * step_count, model_width)
    query_part = jnp.dot(flat_rows, w_query, preferred_element_type=jnp.float32) + b_query.astype(
        jnp.float32
    )
    key_part = jnp.dot(flat_rows, w_key, preferred_element_type=jnp.float32) + b_key.astype(
        jnp.float32
    )
    value_part = jnp.dot(flat_rows, w_value, preferred_element_type=jnp.float32) + b_value.astype(
        jnp.float32
    )
    positions = (lengths[0] + jnp.arange(step_count, dtype=jnp.int32)).astype(jnp.float32)[
        None, :, None
    ]
    query_grid = rotate(
        query_part.reshape(samples, step_count, local_heads, HEAD_DIM), positions
    ).astype(jnp.bfloat16)
    flat_query = query_grid.reshape(samples * step_count, local_heads, HEAD_DIM)
    length_limit = lengths[0]

    def widen_heads(narrow):
        spread_out = narrow.reshape(narrow.shape[:-1] + (KV_HEADS, 1, HEAD_DIM))
        spread_out = jnp.broadcast_to(
            spread_out, narrow.shape[:-1] + (KV_HEADS, group_size, HEAD_DIM)
        )
        return spread_out.reshape(narrow.shape[:-1] + (HEADS * HEAD_DIM,))

    decoded = (
        jnp.full((local_heads, samples * step_count), -jnp.inf, jnp.float32),
        jnp.zeros((local_heads, samples * step_count), jnp.float32),
        jnp.zeros((local_heads, samples * step_count, HEAD_DIM), jnp.float32),
    )
    prefilled = (
        jnp.full((block_count, local_heads, block_width), -jnp.inf, jnp.float32),
        jnp.zeros((block_count, local_heads, block_width), jnp.float32),
        jnp.zeros((block_count, local_heads, block_width, HEAD_DIM), jnp.float32),
    )
    first_query = group_no * block_rows
    stacked = (
        lax.all_gather(prompt_k[None], "grp", axis=0, tiled=True),
        lax.all_gather(prompt_v[None], "grp", axis=0, tiled=True),
    )
    regrouped = (
        lax.all_to_all(prompt_q[None], "tp", split_axis=2, concat_axis=1, tiled=True),
        lax.all_to_all(widen_heads(stacked[0]), "tp", split_axis=2, concat_axis=1, tiled=True),
        lax.all_to_all(widen_heads(stacked[1]), "tp", split_axis=2, concat_axis=1, tiled=True),
    )
    queries = regrouped[0][0].reshape(block_count, block_width, local_heads, HEAD_DIM)
    key_rows = regrouped[1].reshape(-1, local_heads, HEAD_DIM)
    value_rows = regrouped[2].reshape(-1, local_heads, HEAD_DIM)
    prefilled = prefill_sweep(prefilled, queries, first_query, key_rows, value_rows, 0)
    decoded = decode_sweep(decoded, flat_query, key_rows, value_rows, length_limit)
    mixed_rows = prefilled[2] / prefilled[1][..., None]
    mixed_rows = (
        jnp.transpose(mixed_rows, (0, 2, 1, 3))
        .reshape(block_rows, local_heads * HEAD_DIM)
        .astype(jnp.bfloat16)
    )
    prefill_mixed = lax.all_to_all(mixed_rows, "tp", split_axis=0, concat_axis=1, tiled=True)
    split_max = decoded[0].reshape(local_heads, samples, step_count)
    split_sum = decoded[1].reshape(local_heads, samples, step_count)
    split_acc = decoded[2].reshape(local_heads, samples, step_count, HEAD_DIM)
    key_grid = key_part.reshape(samples, step_count, -1)
    value_grid = value_part.reshape(samples, step_count, -1)
    kept_keys = []
    kept_values = []
    produced = []
    for step_no in range(step_count):
        key_piece = key_grid[:, step_no]
        value_piece = value_grid[:, step_no]
        for bit in range(levels):
            other = partner((key_piece, value_piece), "tp", bit)
            upper = tp_no // (1 << bit) % 2 == 1
            key_piece = joined(key_piece, other[0], upper)
            value_piece = joined(value_piece, other[1], upper)
        kv_local = key_piece.shape[-1] // HEAD_DIM
        repeat_by = local_heads // kv_local
        where_at = positions[:, step_no]
        kept_keys.append(
            jnp.repeat(
                rotate(key_piece.reshape(samples, kv_local, HEAD_DIM), where_at).astype(
                    jnp.bfloat16
                ),
                repeat_by,
                axis=1,
            )
        )
        kept_values.append(
            jnp.repeat(
                value_piece.astype(jnp.bfloat16).reshape(samples, kv_local, HEAD_DIM),
                repeat_by,
                axis=1,
            )
        )
        key_stack = jnp.stack(kept_keys, axis=1)
        value_stack = jnp.stack(kept_values, axis=1)
        scores = (
            jnp.einsum(
                "shd,sbhd->hsb",
                query_grid[:, step_no],
                key_stack,
                preferred_element_type=jnp.float32,
            )
            * scaling
        )
        carried = (split_max[:, :, step_no], split_sum[:, :, step_no], split_acc[:, :, step_no])
        carried = absorb(
            carried, scores, jnp.ones(scores.shape, jnp.bool_), value_stack, "hsb,sbhd->hsd"
        )
        attended = (
            jnp.transpose(carried[2] / carried[1][..., None], (1, 0, 2))
            .reshape(samples, local_heads * HEAD_DIM)
            .astype(jnp.bfloat16)
        )
        produced.append(
            lax.psum(jnp.dot(attended, w_out, preferred_element_type=jnp.float32), "tp").astype(
                jnp.bfloat16
            )
        )
    decode_out = jnp.stack(produced, axis=1)
    return (prefill_mixed, decode_out)


def solution(mesh):
    in_specs = (
        P(("grp", "tp"), None),
        P(("grp", "tp"), None),
        P(("grp", "tp"), None),
        P("grp"),
        P("grp", None, None),
        P(),
        P(None, "tp"),
        P("tp"),
        P(None, "tp"),
        P("tp"),
        P(None, "tp"),
        P("tp"),
        P("tp", None),
    )
    out_specs = (P(("grp", "tp"), None), P("grp", None, None))
    return jax.shard_map(shards, mesh=mesh, in_specs=in_specs, out_specs=out_specs, check_vma=False)
```

profile of v0, /device:TPU:14, one launch (start us, length us, event | category | flops | bytes accessed | tf_op | source)
XLA Modules:
  0.0 889.7 jit_solution(8631366954248388733)
XLA Ops:
  7.9 4.9 copy.186
  13.3 23.5 %reduce.26 = bf16[4096,64]{1,0:T(8,128)(2,1)} reduce(bf16[4096,1,64]{2,1,0:T(2,128)(2,1)S(1)} %bitcast.202, bf16[]{:T(256)} %broadcast.474), dimensions={1}, to_apply=%bitcast.142.reduce_sub_computation | reduce | bytes 1048578
  36.8 3.0 reshape.1028
  39.8 10.7 %all-to-all-start = ((bf16[32,2,4096]{2,1,0:T(2,128)(2,1)}), bf16[32,2,4096]{2,1,0:T(2,128)(2,1)}, u32[]{:S(2)}, u32[]{:S(2)}) async-start(bf16[32,2,4096]{2,1,0:T(2,128)(2,1)} %reshape.1028), calls=%async_computation | async-start | bytes 1048576 | tf_op jit(solution)/shard_map/all_to_all | solution.py:175
  51.7 2.5 copy.245
  54.3 2.6 copy.189
  56.9 5.5 broadcast_in_dim.118
  62.4 13.9 %reshape.1030 = bf16[32,2,32768]{2,1,0:T(2,128)(2,1)} reshape(bf16[4096,8,64]{2,1,0:T(8,128)(2,1)} %bitcast.193) | data formatting | bytes 8388608
  76.3 9.2 %all-to-all-start.1 = ((bf16[32,2,32768]{2,1,0:T(2,128)(2,1)}), bf16[32,2,32768]{2,1,0:T(2,128)(2,1)}, u32[]{:S(2)}, u32[]{:S(2)}) async-start(bf16[32,2,32768]{2,1,0:T(2,128)(2,1)} %reshape.1030), calls=%async_computation.1 | async-start | bytes 8388608 | tf_op jit(solution)/shard_map/all_to_all | solution.py:176
  86.3 45.0 %all-gather.7.cloned.1.call-done = bf16[512,1024]{1,0:T(8,128)(2,1)} async-done(((bf16[64,1024]{1,0:T(8,128)(2,1)}), bf16[512,1024]{1,0:T(8,128)(2,1)}) %all-gather.7.cloned.1.call-update) | async-done | bytes 1048592 | tf_op jit(solution)/shard_map/all_gather | solution.py:172
  131.3 2.5 copy.246
  133.8 2.6 copy.192
  136.4 5.5 broadcast_in_dim.121
  141.9 13.9 %reshape.1032 = bf16[32,2,32768]{2,1,0:T(2,128)(2,1)} reshape(bf16[4096,8,64]{2,1,0:T(8,128)(2,1)} %bitcast.194) | data formatting | bytes 8388608
  155.8 27.3 %all-to-all-done.1 = bf16[32,2,32768]{2,1,0:T(2,128)(2,1)} async-done(((bf16[32,2,32768]{2,1,0:T(2,128)(2,1)}), bf16[32,2,32768]{2,1,0:T(2,128)(2,1)}, u32[]{:S(2)}, u32[]{:S(2)}) %all-to-all-start.1) | async-done | bytes 4194336 | tf_op jit(solution)/shard_map/all_to_all | solution.py:176
  183.1 9.2 %all-to-all-start.2 = ((bf16[32,2,32768]{2,1,0:T(2,128)(2,1)}), bf16[32,2,32768]{2,1,0:T(2,128)(2,1)}, u32[]{:S(2)}, u32[]{:S(2)}) async-start(bf16[32,2,32768]{2,1,0:T(2,128)(2,1)} %reshape.1032), calls=%async_computation.2 | async-start | bytes 8388608 | tf_op jit(solution)/shard_map/all_to_all | solution.py:177
  200.7 1.7 collective-permute-start.7
  203.0 1.7 collective-permute-start.5
  205.3 79.4 %collective-permute-done.7 = bf16[16,64]{1,0:T(8,128)(2,1)S(1)} collective-permute-done((bf16[16,64]{1,0:T(8,128)(2,1)S(1)}, bf16[16,64]{1,0:T(8,128)(2,1)S(1)}, u32[]{:S(2)}, u32[]{:S(2)}) %collective-permute-start.7) | collective-permute-done | bytes 2080 | tf_op jit(solution)/shard_map/ppermute | solution.py:18
  285.8 4.1 reshape.1029
  290.0 3.6 copy.187
  295.0 13.7 %reshape.1031 = bf16[4096,8,64]{2,1,0:T(8,128)(2,1)} reshape(bf16[32,2,32768]{2,1,0:T(2,128)(2,1)} %all-to-all-done.1) | data formatting | bytes 8388608
  308.7 9.8 %copy.191 = bf16[8,32,64,128]{3,2,1,0:T(8,128)(2,1)} copy(bf16[8,32,64,128]{2,0,3,1:T(8,128)(2,1)} %bitcast.195) | data formatting | bytes 8388608 | tf_op jit(solution)/shard_map/all_to_all | solution.py:176
  318.5 5.2 select_reduce_fusion
  323.8 13.7 %reshape.1033 = bf16[4096,8,64]{2,1,0:T(8,128)(2,1)} reshape(bf16[32,2,32768]{2,1,0:T(2,128)(2,1)} %all-to-all-done.2) | data formatting | bytes 8388608
  337.5 9.8 %copy.194 = bf16[8,32,64,128]{3,2,1,0:T(8,128)(2,1)} copy(bf16[8,32,64,128]{2,0,3,1:T(8,128)(2,1)} %bitcast.196) | data formatting | bytes 8388608 | tf_op jit(solution)/shard_map/all_to_all | solution.py:177
  347.3 375.3 %while.41 = (s32[]{:T(128)}, f32[4,1,512]{2,0,1:T(4,128)S(1)}, f32[4,1,512,128]{3,2,1,0:T(8,128)}, s32[4]{0:T(128)S(1)}, s32[]{:T(128)}, /*index=5*/bf16[4,512,1...) while((s32[]{:T(128)}, f32[4,1,512]{2,0,1:T(4,128)S(1)}, ...), condition=%wide.region_5.6_spmd, body=%wide.region_0.5_spmd.sunk | while | flops 137498640 | bytes 5171958 | solution.py:85
  348.8 87.1 %while.42 = (s32[]{:T(128)}, f32[1,512]{1,0:T(1,128)S(1)}, f32[1,512]{1,0:T(1,128)S(1)}, f32[1,512,128]{2,1,0:T(8,128)S(1)}, s32[]{:T(128)}, /*index=5*/s32[]{:T...) while((s32[]{:T(128)}, f32[1,512]{1,0:T(1,128)S(1)}, ...), condition=%wide.region_4.4_spmd, body=%wide.region_1.3_spmd.sunk | while | flops 137498624 | bytes 4114627 | solution.py:82
  359.3 1.4 fusion.100
  365.3 1.4 fusion.100
  371.3 1.4 fusion.100
  377.3 1.4 fusion.100
  383.3 1.4 fusion.100
  389.3 1.4 fusion.100
  395.3 1.4 fusion.100
  407.4 1.4 fusion.100
  419.4 1.4 fusion.100
  431.4 1.4 fusion.100
  438.1 90.1 %while.42 = (s32[]{:T(128)}, f32[1,512]{1,0:T(1,128)S(1)}, f32[1,512]{1,0:T(1,128)S(1)}, f32[1,512,128]{2,1,0:T(8,128)S(1)}, s32[]{:T(128)}, /*index=5*/s32[]{:T...) while((s32[]{:T(128)}, f32[1,512]{1,0:T(1,128)S(1)}, ...), condition=%wide.region_4.4_spmd, body=%wide.region_1.3_spmd.sunk | while | flops 137498624 | bytes 4114627 | solution.py:82
  439.6 1.4 fusion.100
  448.6 1.4 fusion.100
  530.4 93.1 %while.42 = (s32[]{:T(128)}, f32[1,512]{1,0:T(1,128)S(1)}, f32[1,512]{1,0:T(1,128)S(1)}, f32[1,512,128]{2,1,0:T(8,128)S(1)}, s32[]{:T(128)}, /*index=5*/s32[]{:T...) while((s32[]{:T(128)}, f32[1,512]{1,0:T(1,128)S(1)}, ...), condition=%wide.region_4.4_spmd, body=%wide.region_1.3_spmd.sunk | while | flops 137498624 | bytes 4114627 | solution.py:82
  625.7 96.1 %while.42 = (s32[]{:T(128)}, f32[1,512]{1,0:T(1,128)S(1)}, f32[1,512]{1,0:T(1,128)S(1)}, f32[1,512,128]{2,1,0:T(8,128)S(1)}, s32[]{:T(128)}, /*index=5*/s32[]{:T...) while((s32[]{:T(128)}, f32[1,512]{1,0:T(1,128)S(1)}, ...), condition=%wide.region_4.4_spmd, body=%wide.region_1.3_spmd.sunk | while | flops 137498624 | bytes 4114627 | solution.py:82
  722.6 2.5 divide_convert_fusion
  725.1 9.4 %all-to-all-start.3 = ((bf16[32,64,128]{2,1,0:T(8,128)(2,1)}), bf16[32,64,128]{2,1,0:T(8,128)(2,1)}, u32[]{:S(2)}, u32[]{:S(2)}) async-start(bf16[32,64,128]{2,1,0:T(8,128)(2,1)} %bitcast.210), calls=%async_computation.3 | async-start | bytes 1048576 | tf_op jit(solution)/shard_map/all_to_all | solution.py:190
  735.5 3.0 convolution_add_fusion.3
  739.9 139.9 %all-reduce.2 = (bf16[16,5120]{1,0:T(8,128)(2,1)S(1)}, bf16[16,5120]{1,0:T(8,128)(2,1)S(1)}) all-reduce(f32[16,5120]{1,0:T(8,128)S(1)} %fusion.52, f32[16,5120]{1,0:T(8,128)S(1)} %fusion.49), channel_id=1, replica_groups=mesh['grp'=8,'tp'=32] {'tp'}, use_global_device_ids=true, to_apply=%region_12.13 | all-reduce | flops 163840 | bytes 983040 | tf_op jit(solution)/shard_map/psum | solution.py:247
  881.0 1.9 copy_bitcast_fusion
  (978 shorter events, 365.5 us)
Async XLA Ops:
  7.2 732.1 %copy-start = (bf16[128,5120]{1,0:T(8,128)(2,1)S(1)}, bf16[128,5120]{1,0:T(8,128)(2,1)}, u32[]{:S(2)}) copy-start(bf16[128,5120]{1,0:T(8,128)(2,1)} %param.29) | copy-start | bytes 3932164
  7.2 44.6 %all-gather.5.cloned.1.call-start = ((), (), s32[]{:S(2)}) async-start(), calls=%async_computation.4 | async-start | bytes 1179648 | tf_op jit(solution)/shard_map/all_gather | solution.py:171
  39.8 36.5 %all-to-all-start = ((bf16[32,2,4096]{2,1,0:T(2,128)(2,1)}), bf16[32,2,4096]{2,1,0:T(2,128)(2,1)}, u32[]{:S(2)}, u32[]{:S(2)}) async-start(bf16[32,2,4096]{2,1,0:T(2,128)(2,1)} %reshape.1028), calls=%async_computation | async-start | bytes 1048576 | tf_op jit(solution)/shard_map/all_to_all | solution.py:175
  76.3 106.9 %all-to-all-start.1 = ((bf16[32,2,32768]{2,1,0:T(2,128)(2,1)}), bf16[32,2,32768]{2,1,0:T(2,128)(2,1)}, u32[]{:S(2)}, u32[]{:S(2)}) async-start(bf16[32,2,32768]{2,1,0:T(2,128)(2,1)} %reshape.1030), calls=%async_computation.1 | async-start | bytes 8388608 | tf_op jit(solution)/shard_map/all_to_all | solution.py:176
  85.5 45.8 %all-gather.7.cloned.1.call-start = ((), (), s32[]{:S(2)}) async-start(), calls=%async_computation.5 | async-start | bytes 1179648 | tf_op jit(solution)/shard_map/all_gather | solution.py:172
  155.8 36.6 %copy-start.4 = (bf16[5120]{0:T(1024)(128)(2,1)S(1)}, bf16[5120]{0:T(1024)(128)(2,1)}, u32[]{:S(2)}) copy-start(bf16[5120]{0:T(1024)(128)(2,1)} %param.22) | copy-start | bytes 30724
  155.8 36.7 %copy-start.3 = (bf16[16,2,5120]{2,1,0:T(2,128)(2,1)S(1)}, bf16[16,2,5120]{2,1,0:T(2,128)(2,1)}, u32[]{:S(2)}) copy-start(bf16[16,2,5120]{2,1,0:T(2,128)(2,1)} %param.21) | copy-start | bytes 983044
  155.8 37.6 %copy-start.5 = (bf16[32]{0:T(256)(128)(2,1)S(1)}, bf16[32]{0:T(256)(128)(2,1)}, u32[]{:S(2)}) copy-start(bf16[32]{0:T(256)(128)(2,1)} %param.26) | copy-start | bytes 196
  183.1 140.7 %all-to-all-start.2 = ((bf16[32,2,32768]{2,1,0:T(2,128)(2,1)}), bf16[32,2,32768]{2,1,0:T(2,128)(2,1)}, u32[]{:S(2)}, u32[]{:S(2)}) async-start(bf16[32,2,32768]{2,1,0:T(2,128)(2,1)} %reshape.1032), calls=%async_computation.2 | async-start | bytes 8388608 | tf_op jit(solution)/shard_map/all_to_all | solution.py:177
  192.4 2.9 copy-start.6
  192.4 5.4 copy-start.7
  192.4 5.5 copy-start.2
  194.7 8.2 collective-permute-start.4
  195.0 9.7 %collective-permute-start = (f32[16,32]{1,0:T(8,128)S(1)}, f32[16,32]{1,0:T(8,128)S(1)}, u32[]{:S(2)}, u32[]{:S(2)}) collective-permute-start(f32[16,32]{1,0:T(8,128)S(1)} %bitcast.239), channel_id=1, source_target_pairs={{0,1},{1,0},{2,3},{3,2},{4,5},{5,4},{6,7},{7,6},{8,9},{9,8},{10,11... | collective-permute-start | bytes 6152 | tf_op jit(solution)/shard_map/ppermute | solution.py:18
  196.5 4.1 collective-permute-start.6
  196.8 5.6 collective-permute-start.2
  200.7 84.0 %collective-permute-start.7 = (bf16[16,64]{1,0:T(8,128)(2,1)S(1)}, bf16[16,64]{1,0:T(8,128)(2,1)S(1)}, u32[]{:S(2)}, u32[]{:S(2)}) collective-permute-start(bf16[16,64]{1,0:T(8,128)(2,1)S(1)} %maximum_select_fusion.7), channel_id=1, source_target_pairs={{0,2},{1,3},{2,0},{3,1},{4,6},{5,7},{6,4},{7,5},{8,10},{9,11},{10,... | collective-permute-start | bytes 6152 | tf_op jit(solution)/shard_map/ppermute | solution.py:18
  202.5 82.3 %collective-permute-start.3 = (bf16[16,64]{1,0:T(8,128)(2,1)S(1)}, bf16[16,64]{1,0:T(8,128)(2,1)S(1)}, u32[]{:S(2)}, u32[]{:S(2)}) collective-permute-start(bf16[16,64]{1,0:T(8,128)(2,1)S(1)} %maximum_select_fusion.2), channel_id=1, source_target_pairs={{0,2},{1,3},{2,0},{3,1},{4,6},{5,7},{6,4},{7,5},{8,10},{9,11},{10,... | collective-permute-start | bytes 6152 | tf_op jit(solution)/shard_map/ppermute | solution.py:18
  203.0 82.0 %collective-permute-start.5 = (f32[16,64]{1,0:T(8,128)S(1)}, f32[16,64]{1,0:T(8,128)S(1)}, u32[]{:S(2)}, u32[]{:S(2)}) collective-permute-start(f32[16,64]{1,0:T(8,128)S(1)} %maximum_select_fusion.4), channel_id=1, source_target_pairs={{0,2},{1,3},{2,0},{3,1},{4,6},{5,7},{6,4},{7,5},{8,10},{9,11},{10,... | collective-permute-start | bytes 12296 | tf_op jit(solution)/shard_map/ppermute | solution.py:18
  204.8 80.2 %collective-permute-start.1 = (f32[16,64]{1,0:T(8,128)S(1)}, f32[16,64]{1,0:T(8,128)S(1)}, u32[]{:S(2)}, u32[]{:S(2)}) collective-permute-start(f32[16,64]{1,0:T(8,128)S(1)} %maximum_select_fusion), channel_id=1, source_target_pairs={{0,2},{1,3},{2,0},{3,1},{4,6},{5,7},{6,4},{7,5},{8,10},{9,11},{10,... | collective-permute-start | bytes 12296 | tf_op jit(solution)/shard_map/ppermute | solution.py:18
  722.6 12.2 %copy-start.1 = (f32[32,16384]{1,0:T(8,128)S(1)}, f32[32,16384]{1,0:T(8,128)}, u32[]{:S(2)}) copy-start(f32[32,16384]{1,0:T(8,128)} %get-tuple-element.282) | copy-start | bytes 6291460
  725.1 155.9 %all-to-all-start.3 = ((bf16[32,64,128]{2,1,0:T(8,128)(2,1)}), bf16[32,64,128]{2,1,0:T(8,128)(2,1)}, u32[]{:S(2)}, u32[]{:S(2)}) async-start(bf16[32,64,128]{2,1,0:T(8,128)(2,1)} %bitcast.210), calls=%async_computation.3 | async-start | bytes 1048576 | tf_op jit(solution)/shard_map/all_to_all | solution.py:190
Sparse Core Ops, SparseCore 0:
  9.8 41.8 all-gather.4
  88.1 43.1 all-gather.6
where the time goes:
time: 897 us; the launch traced here: 890 us
  matrix products  338 us (38%)
  waiting for transfers between devices  154 us (17%)
  blocking collectives  140 us (16%)
  local copies, waits for them, and re-layouts  124 us (14%)
  other arithmetic  63.6 us (7%)
  starting transfers between devices  44.5 us (5%)
  between operations  15.2 us (2%)
  loops' own time  10.2 us (1%)
    dot_general x124, matrix products, absorb(): jnp.einsum(pattern, weights.astype(jnp.bfloat16), values, preferred_eleme...  179 us
    dot_general x122, matrix products, visit_block(): jnp.einsum('qhd,khd->hqk', query_block, key_block, preferred_element_type...  150 us
    psum x1, blocking collectives, shards(): lax.psum(jnp.dot(attended, w_out, preferred_element_type=jnp.float32), 'tp')  140 us
    ppermute x8, waiting for transfers between devices, partner(): lax.ppermute(value, axis, [(i, i ^ 1 << stride) for i in range(lax.axis_s...  79.4 us
    unnamed x27, local copies, waits for them, and re-layouts  70 us
    all_gather x1, waiting for transfers between devices, shards(): lax.all_gather(prompt_v[None], 'grp', axis=0, tiled=True)  45 us
    reduce_sum x124, other arithmetic, absorb(): row_sum = row_sum * shrink + jnp.sum(weights, axis=-1)  30.1 us
    all_to_all x1, waiting for transfers between devices, shards(): lax.all_to_all(widen_heads(stacked[0]), 'tp', split_axis=2, concat_axis=1...  27.3 us
  transfers between devices with their start and end apart: 14, of which 4 were waited for; matrix products, arithmetic and copies ran while one was open for 15% of the time, Pallas kernels for 0%

commit v1 on v0

v1 whole, which is shorter than its diff:
```python
import math

import jax
import jax.numpy as jnp
from jax import lax
from jax.experimental import pallas as pl
from jax.experimental.pallas import tpu as pltpu
from jax.sharding import PartitionSpec as P

HEADS = 32
KV_HEADS = 8
HEAD_DIM = 128
STEPS = 2
EPSILON = 1e-06
ROPE_BASE = 1000000.0
MESH = pl.DeviceIdType.MESH
F32 = jnp.float32
BF16 = jnp.bfloat16
NEG = -1e30
C = math.log2(math.e) / math.sqrt(HEAD_DIM)
NT = (((1,), (1,)), ((), ()))
CHUNK = 1024
TILE = 256


def dot_nt(a, b):
    return lax.dot_general(a, b, NT, preferred_element_type=F32)


def kernel(
    q_ref, k_ref, v_ref, st_ref, gain_ref, cos_ref, sin_ref, len_ref,
    wq_ref, bq_ref, wk_ref, bk_ref, wv_ref, bv_ref, wo_ref,
    out_ref, dec_ref,
    kvbuf, qbuf, obuf, S, acc, mx, ls,
    wq_v, wk_v, wv_v, wo_v, dq_own, dq, kvp_own, kvp, pmsg, part, opart, rs0, hsum, rs, fbuf, fsib,
    dacc, dmx, dls,
    w_sem, kv0_recv, kv0_loc, kv0_send, q_recv, q_send, ag_recv, ag_send, sib_recv, sib_send,
    o_recv, o_send, dq_recv, dq_send, kvp_recv, kvp_send, part_recv, part_send,
    rs0_recv, rs0_send, rs_recv, rs_send, f_recv, f_send, fs_recv, fs_send,
):
    g = lax.axis_index("grp")
    t = lax.axis_index("tp")
    x, ylo = lax.rem(g, 4), lax.div(g, 4)
    yhi, z, core = lax.div(t, 16), lax.rem(lax.div(t, 2), 8), lax.rem(t, 2)
    y = yhi * 2 + ylo
    own = (ylo * 4 + x) * 2 + yhi

    def dev(xx, yy, zz, cc):
        return {"grp": lax.rem(yy, 2) * 4 + xx, "tp": lax.div(yy, 2) * 16 + zz * 2 + cc}

    def flip(bit, by):
        return bit + by * (1 - 2 * bit)

    def column(by):
        return x + by * (3 - 2 * x), y + by * (3 - 2 * y)

    def rcopy(src, dst, send, recv, to):
        return pltpu.make_async_remote_copy(
            src_ref=src, dst_ref=dst, send_sem=send, recv_sem=recv, device_id=to, device_id_type=MESH
        )

    def drain(ref, sem):
        pltpu.make_async_copy(ref, ref, sem).wait()

    def head_cols(ref, h, width=HEAD_DIM):
        return ref.at[:, pl.ds(pl.multiple_of(h * width, width), width)]

    weights = [
        pltpu.make_async_copy(a, b, w_sem.at[i])
        for i, (a, b) in enumerate(((wq_ref, wq_v), (wk_ref, wk_v), (wv_ref, wv_v), (wo_ref, wo_v)))
    ]
    for w in weights:
        w.start()

    barrier = pltpu.get_barrier_semaphore()

    def greet(to):
        pl.semaphore_signal(barrier, inc=1, device_id=to, device_id_type=MESH)

    y2 = lax.rem(y + 2, 4)
    for dc in range(2):
        for dz in range(8):
            zz, cc = lax.rem(z + dz, 8), flip(core, dc)
            if dz or dc:
                greet(dev(x, y, zz, cc))
            greet(dev(3 - x, 3 - y, zz, cc))
            greet(dev(x, y2, zz, cc))
    for d in (1, 3):
        greet(dev(lax.rem(x + d, 4), y, z, core))
        greet(dev(x, lax.rem(y + d, 4), z, core))
    pl.semaphore_wait(barrier, 51)

    for dz in range(1, 8):
        zz = lax.rem(z + dz, 8)
        for kv, ref in enumerate((k_ref, v_ref)):
            rcopy(
                head_cols(ref, zz), kvbuf.at[kv, own, z, core], kv0_send.at[kv], kv0_recv.at[kv],
                dev(x, y, zz, core),
            ).start()
    kv_local = [
        pltpu.make_async_copy(head_cols(ref, z), kvbuf.at[kv, own, z, core], kv0_loc.at[kv])
        for kv, ref in enumerate((k_ref, v_ref))
    ]
    for c in kv_local:
        c.start()
    for dz in range(8):
        zz = lax.rem(z + dz, 8)
        for dp in range(2):
            px, py = column(dp)
            for dc in range(2):
                cc = flip(core, dc)
                src = head_cols(q_ref, 4 * zz + 2 * flip(ylo, dp) + cc)
                dst = qbuf.at[ylo, z, core]
                if dz or dp or dc:
                    rcopy(src, dst, q_send.at[dp], q_recv.at[ylo], dev(px, py, zz, cc)).start()
                else:
                    pltpu.make_async_copy(src, dst, q_recv.at[ylo]).start()

    states = st_ref[...].astype(F32)
    scale = lax.rsqrt(jnp.mean(states * states, axis=1, keepdims=True) + EPSILON)
    normed = (states * scale * gain_ref[...].astype(F32)).astype(BF16)
    for w in weights:
        w.wait()
    cosine, sine = cos_ref[...], sin_ref[...]

    def rotate(value):
        return value * cosine + pltpu.roll(value, HEAD_DIM // 2, 1) * sine

    query = jnp.dot(normed, wq_v[...], preferred_element_type=F32) + bq_ref[...].astype(F32)
    dq_own[...] = rotate(query).astype(BF16)
    quarter = lax.rem(t, 4)
    spread = (
        lax.broadcasted_iota(jnp.int32, (32, HEAD_DIM), 1)
        == lax.broadcasted_iota(jnp.int32, (32, HEAD_DIM), 0) + quarter * 32
    ).astype(F32)
    for i, (w, b) in enumerate(((wk_v, bk_ref), (wv_v, bv_ref))):
        narrow = jnp.dot(normed, w[...], preferred_element_type=F32) + b[...].astype(F32)
        kvp_own[i] = jnp.dot(narrow, spread, precision=lax.Precision.HIGHEST, preferred_element_type=F32)

    late = []

    def to_tp(target, src, dst, send, recv):
        @pl.when(target != t)
        def _():
            rcopy(src, dst, send, recv, {"grp": g, "tp": target}).start()

        @pl.when(target == t)
        def _():
            pltpu.make_async_copy(src, dst, recv).start()

        late.append((target, src, send))

    for i in range(4):
        target = (i // 2) * 16 + lax.div(t, 4) * 2 + i % 2
        to_tp(target, dq_own, dq.at[quarter], dq_send.at[i], dq_recv.at[quarter])
    for m in range(1, 4):
        target = lax.div(t, 4) * 4 + lax.rem(quarter + m, 4)
        rcopy(kvp_own, kvp.at[m - 1], kvp_send.at[m - 1], kvp_recv.at[m - 1], {"grp": g, "tp": target}).start()

    def place(o1, o2):
        ox, oy = (1 - core) * o1 + core * o2, core * o1 + (1 - core) * o2
        return lax.rem(x + ox, 4), lax.rem(y + oy, 4)

    def chunk_of(o1, o2):
        xx, yy = place(o1, o2)
        return (lax.rem(yy, 2) * 4 + xx) * 2 + lax.div(yy, 2)

    def block(o1, o2, kv=None):
        return kvbuf.at[slice(None) if kv is None else kv, chunk_of(o1, o2), :, core]

    def toward(axis, step):
        xx, yy = place(step, 0) if axis == 1 else place(0, step)
        return dev(xx, yy, z, core)

    sends = []

    def send(src, sem, recv, to):
        c = rcopy(src, src, sem, recv, to)
        c.start()
        sends.append(c)

    sibling = dev(x, y, z, 1 - core)

    def to_sibling(o1, o2):
        send(block(o1, o2), sib_send.at[o1, o2], sib_recv.at[o1, o2], sibling)

    def from_sibling(o1, o2):
        drain(kvbuf.at[:, chunk_of(o1, o2), :, 1 - core], sib_recv.at[o2, o1])

    def open_axis1():
        send(block(0, 0), ag_send.at[0, 0], ag_recv.at[3, 0, 0], toward(1, 1))
        send(block(0, 0), ag_send.at[0, 1], ag_recv.at[1, 0, 0], toward(1, 3))

    def open_axis2(o1):
        send(block(o1, 0), ag_send.at[1 + o1, 0], ag_recv.at[o1, 3, 0], toward(2, 1))
        send(block(o1, 0), ag_send.at[1 + o1, 1], ag_recv.at[o1, 1, 0], toward(2, 3))

    def pass_axis1():
        drain(block(3, 0), ag_recv.at[3, 0, 0])
        send(block(3, 0, 0), ag_send.at[0, 2], ag_recv.at[2, 0, 0], toward(1, 1))
        drain(block(1, 0), ag_recv.at[1, 0, 0])
        send(block(1, 0, 1), ag_send.at[0, 3], ag_recv.at[2, 0, 1], toward(1, 3))

    def pass_axis2(o1):
        drain(block(o1, 3), ag_recv.at[o1, 3, 0])
        send(block(o1, 3, 0), ag_send.at[1 + o1, 2], ag_recv.at[o1, 2, 0], toward(2, 1))
        drain(block(o1, 1), ag_recv.at[o1, 1, 0])
        send(block(o1, 1, 1), ag_send.at[1 + o1, 3], ag_recv.at[o1, 2, 1], toward(2, 3))
        to_sibling(o1, 3)
        to_sibling(o1, 1)

    def end_axis(o1, o2):
        for kv in range(2):
            drain(block(o1, o2, kv), ag_recv.at[o1, o2, kv])
        to_sibling(o1, o2)

    for kv in range(2):
        kv_local[kv].wait()
        drain(kvbuf.at[kv, own, pl.ds(0, 7), core], kv0_recv.at[kv])
    open_axis1()
    open_axis2(0)
    to_sibling(0, 0)
    pass_axis1()
    open_axis2(1)
    open_axis2(3)
    to_sibling(1, 0)
    to_sibling(3, 0)
    pass_axis2(0)
    end_axis(2, 0)
    open_axis2(2)
    pass_axis2(1)
    pass_axis2(3)
    end_axis(0, 2)
    pass_axis2(2)
    end_axis(1, 2)
    end_axis(3, 2)
    end_axis(2, 2)
    for o1 in range(4):
        for o2 in range(4):
            from_sibling(o1, o2)

    for slot in range(2):
        drain(qbuf.at[slot], q_recv.at[slot])
    acc[...] = jnp.zeros_like(acc)
    mx[...] = jnp.full_like(mx, NEG)
    ls[...] = jnp.zeros_like(ls)
    low = own + ylo * (15 - 2 * own)

    def unit(slot, cc, diagonal):
        tiles = CHUNK // TILE
        keys = kvbuf[0, cc].reshape(CHUNK, HEAD_DIM)
        values = kvbuf[1, cc].reshape(CHUNK, HEAD_DIM)
        held = {}

        def scores(i):
            width = (i + 1) * TILE if diagonal else CHUNK
            rows = pl.ds(i * TILE, TILE)
            s = dot_nt(qbuf[slot, 2 * i : 2 * i + 2].reshape(TILE, HEAD_DIM), keys[:width])
            if diagonal:
                r = lax.broadcasted_iota(jnp.int32, (TILE, width), 0) + i * TILE
                s = jnp.where(lax.broadcasted_iota(jnp.int32, (TILE, width), 1) <= r, s, NEG)
            S[i % 2, :, :width] = s
            old = mx[slot, rows, :]
            new = jnp.maximum(old, jnp.max(s, axis=1, keepdims=True))
            mx[slot, rows, :] = new
            held[i] = (old, new)

        def mix(i):
            width = (i + 1) * TILE if diagonal else CHUNK
            rows = pl.ds(i * TILE, TILE)
            old, new = held.pop(i)
            p = jnp.exp2(S[i % 2, :, :width] * C - (new * C)[:, :1])
            shrink = jnp.exp2((old - new) * C)
            ls[slot, rows, :] = ls[slot, rows, :] * shrink + jnp.sum(p, axis=1, keepdims=True)
            gained = jnp.dot(p.astype(BF16), values[:width], preferred_element_type=F32)
            acc[slot, rows, :] = acc[slot, rows, :] * shrink + gained

        scores(0)
        for i in range(tiles):
            if i + 1 < tiles:
                scores(i + 1)
            mix(i)

    def visit(i, carry):
        cc, slot = lax.div(i, 2), lax.rem(i, 2)
        last = low + slot * (15 - 2 * low)

        @pl.when(cc < last)
        def _():
            unit(slot, cc, False)

        @pl.when(cc == last)
        def _():
            unit(slot, cc, True)

        return carry

    lax.fori_loop(0, 32, visit, 0)

    for slot in range(2):
        obuf[slot] = (acc[slot] / ls[slot]).astype(BF16).reshape(8, 2, 64, HEAD_DIM)
        dp = flip(slot, ylo)
        px, py = column(dp)
        for dz in range(8):
            zz = lax.rem(z + dz, 8)
            for dc in range(2):
                cc = flip(core, dc)
                src = obuf.at[slot, zz, cc]
                dst = head_cols(out_ref, 4 * z + 2 * ylo + core)

                def away(src=src, dst=dst, to=dev(px, py, zz, cc), dp=dp):
                    rcopy(src, dst, o_send.at[dp], o_recv, to).start()

                if dz or dc:
                    away()
                else:
                    pl.when(dp == 1)(away)

                    @pl.when(dp == 0)
                    def _():
                        pltpu.make_async_copy(src, dst, o_recv).start()

    for i in range(4):
        drain(dq.at[i], dq_recv.at[i])
    dacc[...] = jnp.zeros_like(dacc)
    dmx[...] = jnp.full_like(dmx, NEG)
    dls[...] = jnp.zeros_like(dls)
    limit = len_ref[0]
    yq = lax.rem(y + core, 4)

    def decode_visit(i, carry):
        cc = (lax.rem(yq, 2) * 4 + i) * 2 + lax.div(yq, 2)
        s = dot_nt(dq[...].reshape(128, HEAD_DIM), kvbuf[0, cc].reshape(CHUNK, HEAD_DIM))
        allowed = lax.broadcasted_iota(jnp.int32, (128, CHUNK), 1) + cc * CHUNK < limit
        s = jnp.where(allowed, s, NEG)
        old = dmx[...]
        new = jnp.maximum(old, jnp.max(s, axis=1, keepdims=True))
        dmx[...] = new
        p = jnp.where(allowed, jnp.exp2(s * C - (new * C)[:, :1]), 0.0)
        shrink = jnp.exp2((old - new) * C)
        dls[...] = dls[...] * shrink + jnp.sum(p, axis=1, keepdims=True)
        gained = jnp.dot(
            p.astype(BF16), kvbuf[1, cc].reshape(CHUNK, HEAD_DIM), preferred_element_type=F32
        )
        dacc[...] = dacc[...] * shrink + gained
        return carry

    lax.fori_loop(0, 4, decode_visit, 0)
    first = lax.broadcasted_iota(jnp.int32, (32, HEAD_DIM), 1) < 64
    for i in range(4):
        rows = pl.ds(i * 32, 32)
        pmsg[i, 0] = dacc[rows, :]
        pmsg[i, 1] = jnp.where(first, dmx[rows, :], dls[rows, :])
    for i in range(4):
        slot = yhi * 2 + core
        to_tp(4 * z + i, pmsg.at[i], part.at[slot], part_send.at[i], part_recv.at[slot])

    for i in range(4):
        drain(part.at[i], part_recv.at[i])
    for i in range(3):
        drain(kvp.at[i], kvp_recv.at[i])
    step_key = rotate(kvp_own[0] + kvp[0, 0] + kvp[1, 0] + kvp[2, 0]).astype(BF16).astype(F32)
    step_value = (kvp_own[1] + kvp[0, 1] + kvp[1, 1] + kvp[2, 1]).astype(BF16).astype(F32)
    step_query = dq_own[...].astype(F32)
    here = jnp.sum(step_query * step_key, axis=1, keepdims=True)
    before = jnp.sum(step_query * pltpu.roll(step_key, 1, 0), axis=1, keepdims=True)
    later = lax.rem(lax.broadcasted_iota(jnp.int32, (32, 1), 0), 2) == 1
    before = jnp.where(later, before, NEG)
    tops = [part[i, 1][:, :1] for i in range(4)]
    sums = [part[i, 1][:, 64:65] for i in range(4)]
    top = jnp.maximum(here, before)
    for m in tops:
        top = jnp.maximum(top, m)
    p_here = jnp.exp2((here - top) * C)
    p_before = jnp.where(later, jnp.exp2((before - top) * C), 0.0)
    total = p_here + p_before
    mixed = p_here.astype(BF16).astype(F32) * step_value
    mixed = mixed + p_before.astype(BF16).astype(F32) * pltpu.roll(step_value, 1, 0)
    for i in range(4):
        w = jnp.exp2((tops[i] - top) * C)
        total = total + w * sums[i]
        mixed = mixed + w * part[i, 0]
    attended = (mixed / total).astype(BF16)
    half = wo_v.shape[1] // 2
    for i in range(2):
        opart[i] = jnp.dot(attended, wo_v[:, i * half : (i + 1) * half], preferred_element_type=F32)

    c = rcopy(opart.at[1 - core], rs0, rs0_send, rs0_recv, sibling)
    c.start()
    sends.append(c)
    drain(rs0, rs0_recv)
    hsum[...] = opart[core] + rs0[...]

    def slab(ref, n):
        rows = pl.ds(pl.multiple_of(lax.div(n, 4) * 8, 8), 8)
        return ref.at[rows, pl.ds(pl.multiple_of(lax.rem(n, 4) * 640, 128), 640)]

    mine = yhi * 8 + z
    for n in range(16):
        zz, yy = lax.rem(z + n % 8, 8), flip(yhi, n // 8)
        src = slab(hsum, yy * 8 + zz)
        if n:
            rcopy(src, rs.at[n], rs_send.at[n], rs_recv.at[n], dev(x, yy * 2 + ylo, zz, core)).start()
        else:
            pltpu.make_async_copy(src, rs.at[0], rs_recv.at[0]).start()
    for n in range(16):
        drain(rs.at[n], rs_recv.at[n])
    total_rows = rs[0]
    for n in range(1, 16):
        total_rows = total_rows + rs[n]
    rs[0] = total_rows
    for n in range(16):
        zz, yy = lax.rem(z + n % 8, 8), flip(yhi, n // 8)
        if n:
            rcopy(rs.at[0], slab(fbuf, mine), f_send.at[n], f_recv, dev(x, yy * 2 + ylo, zz, core)).start()
        else:
            pltpu.make_async_copy(rs.at[0], slab(fbuf, mine), f_recv).start()
    drain(fbuf, f_recv)
    c = rcopy(fbuf, fsib, fs_send, fs_recv, sibling)
    c.start()
    sends.append(c)
    drain(fsib, fs_recv)
    dec_ref[core] = fbuf[...].astype(BF16)
    dec_ref[1 - core] = fsib[...].astype(BF16)

    for n in range(1, 16):
        drain(rs.at[n], rs_send.at[n])
        drain(rs.at[n], f_send.at[n])
    for target, src, sem in late:
        pl.when(target != t)(lambda src=src, sem=sem: drain(src, sem))
    for i in range(3):
        drain(kvp_own, kvp_send.at[i])
    for kv in range(2):
        drain(kvbuf.at[0, pl.ds(0, 7), 0, 0], kv0_send.at[kv])
    drain(kvbuf.at[0, pl.ds(0, 15), 0, 0], q_send.at[0])
    drain(kvbuf.at[0, pl.ds(0, 16), 0, 0], q_send.at[1])
    drain(kvbuf.at[0, pl.ds(0, 15), 0, 0], o_send.at[0])
    drain(kvbuf.at[0, pl.ds(0, 16), 0, 0], o_send.at[1])
    for c in sends:
        c.wait_send()
    drain(out_ref, o_recv)


def shards(
    prompt_q, prompt_k, prompt_v, lengths, sample_states, norm_gain,
    w_query, b_query, w_key, b_key, w_value, b_value, w_out,
):
    samples, steps, width = sample_states.shape
    rows = samples * steps
    half_dim = HEAD_DIM // 2
    positions = (lengths[0] + jnp.arange(steps, dtype=jnp.int32)).astype(F32)[:, None]
    frequency = ROPE_BASE ** (-(2.0 * jnp.arange(half_dim, dtype=F32)) / HEAD_DIM)
    angles = positions * frequency
    cosine, sine = jnp.cos(angles), jnp.sin(angles)
    cosine = jnp.tile(jnp.concatenate([cosine, cosine], axis=1), (samples, 1))
    sine = jnp.tile(jnp.concatenate([-sine, sine], axis=1), (samples, 1))
    vmem = pl.BlockSpec(memory_space=pltpu.VMEM)
    smem = pl.BlockSpec(memory_space=pltpu.SMEM)
    hbm = pl.BlockSpec(memory_space=pl.ANY)
    dma = pltpu.SemaphoreType.DMA
    half = width // 2
    prefill, decoded = pl.pallas_call(
        kernel,
        out_shape=(
            jax.ShapeDtypeStruct(prompt_q.shape, BF16),
            jax.ShapeDtypeStruct((2, rows, half), BF16),
        ),
        in_specs=[hbm, hbm, hbm, vmem, vmem, vmem, vmem, smem, hbm, vmem, hbm, vmem, hbm, vmem, hbm],
        out_specs=(hbm, vmem),
        scratch_shapes=[
            pltpu.VMEM((2, 16, 8, 2, 64, HEAD_DIM), BF16),
            pltpu.VMEM((2, 8, 2, 64, HEAD_DIM), BF16),
            pltpu.VMEM((2, 8, 2, 64, HEAD_DIM), BF16),
            pltpu.VMEM((2, TILE, CHUNK), F32),
            pltpu.VMEM((2, CHUNK, HEAD_DIM), F32),
            pltpu.VMEM((2, CHUNK, HEAD_DIM), F32),
            pltpu.VMEM((2, CHUNK, HEAD_DIM), F32),
            pltpu.VMEM(w_query.shape, BF16),
            pltpu.VMEM(w_key.shape, BF16),
            pltpu.VMEM(w_value.shape, BF16),
            pltpu.VMEM(w_out.shape, BF16),
            pltpu.VMEM((rows, HEAD_DIM), BF16),
            pltpu.VMEM((4, rows, HEAD_DIM), BF16),
            pltpu.VMEM((2, rows, HEAD_DIM), F32),
            pltpu.VMEM((3, 2, rows, HEAD_DIM), F32),
            pltpu.VMEM((4, 2, rows, HEAD_DIM), F32),
            pltpu.VMEM((4, 2, rows, HEAD_DIM), F32),
            pltpu.VMEM((2, rows, half), F32),
            pltpu.VMEM((rows, half), F32),
            pltpu.VMEM((rows, half), F32),
            pltpu.VMEM((16, 8, 640), F32),
            pltpu.VMEM((rows, half), F32),
            pltpu.VMEM((rows, half), F32),
            pltpu.VMEM((4 * rows, HEAD_DIM), F32),
            pltpu.VMEM((4 * rows, HEAD_DIM), F32),
            pltpu.VMEM((4 * rows, HEAD_DIM), F32),
            dma((4,)),
            dma((2,)), dma((2,)), dma((2,)),
            dma((2,)), dma((2,)),
            dma((4, 4, 2)), dma((5, 4)), dma((4, 4)), dma((4, 4)),
            dma, dma((2,)),
            dma((4,)), dma((4,)),
            dma((3,)), dma((3,)),
            dma((4,)), dma((4,)),
            dma, dma, dma((16,)), dma((16,)), dma, dma((16,)), dma, dma,
        ],
        compiler_params=pltpu.CompilerParams(
            collective_id=0, has_side_effects=True, vmem_limit_bytes=56 * 2**20
        ),
    )(
        prompt_q, prompt_k, prompt_v, sample_states.reshape(rows, width), norm_gain[None],
        cosine, sine, lengths, w_query, b_query[None], w_key, b_key[None], w_value, b_value[None], w_out,
    )
    decode_out = jnp.concatenate([decoded[0], decoded[1]], axis=1).reshape(samples, steps, width)
    return prefill, decode_out


def solution(mesh):
    in_specs = (
        P(("grp", "tp"), None),
        P(("grp", "tp"), None),
        P(("grp", "tp"), None),
        P("grp"),
        P("grp", None, None),
        P(),
        P(None, "tp"),
        P("tp"),
        P(None, "tp"),
        P("tp"),
        P(None, "tp"),
        P("tp"),
        P("tp", None),
    )
    out_specs = (P(("grp", "tp"), None), P("grp", None, None))
    return jax.shard_map(shards, mesh=mesh, in_specs=in_specs, out_specs=out_specs, check_vma=False)
```

time: 897 us -> 141 us (0.16)
  the two profiles are of different devices: /device:TPU:14 before, /device:TPU:25 now
where the time goes in v1:
time: 141 us; the launch traced here: 140 us
  Pallas kernels  127 us (90%)
  local copies, waits for them, and re-layouts  9.98 us (7%)
    pallas_call x1, Pallas kernels, shards(): pl.pallas_call(kernel, out_shape=(jax.ShapeDtypeStruct(prompt_q.shape, BF...  127 us
    unnamed x7, local copies, waits for them, and re-layouts  4.42 us

profile of v1, /device:TPU:25, one launch (start us, length us, event | category | flops | bytes accessed | tf_op | source)
XLA Modules:
  0.0 140.1 jit_solution(15673055965396400236)
XLA Ops:
  0.6 0.0 copy-start.1
  1.4 0.1 fusion
  1.5 0.1 pad_maximum_fusion.1
  1.5 0.6 tile.8
  2.2 0.6 tile.20
  2.8 1.3 broadcast_in_dim.14.gain_ref
  4.1 1.8 %reshape.32.st_ref = bf16[32,5120]{1,0:T(8,128)(2,1)} reshape(bf16[16,2,5120]{2,1,0:T(2,128)(2,1)} %param.17) | data formatting | bytes 655360 | tf_op jit(solution)/shard_map/reshape | solution.py:511
  5.9 2.2 %copy.15.wk_ref = bf16[5120,32]{1,0:T(8,128)(2,1)} copy(bf16[5120,32]{0,1:T(8,128)(2,1)} %param.21) | data formatting | bytes 655360 | tf_op args[8]
  8.2 0.0 copy-done.1
  8.2 1.4 copy.16.wv_ref
  9.5 127.5 %shard_map.140 = (bf16[64,4096]{1,0:T(8,128)(2,1)}, bf16[2,32,2560]{2,1,0:T(8,128)(2,1)}) custom-call(bf16[64,4096]{1,0:T(8,128)(2,1)} %q_ref.1, bf16[64,1024]{1,0:T(8,128)(2,1)} %k_ref.1, bf16[64,1024]{1,0:T(8,128)(2,1)} %v_ref.1, bf16[32,5120]{1,0:T(8,128)(2,1)} %reshape.32.st_ref, bf16[1,5120]{1,0:T(2,128)(2,1)} %broadcast_in_dim.14.gain_ref, ...), custom_call_target="tpu_custom_call" | custom-call | tf_op jit(solution)/shard_map/pallas_call | solution.py:462
  137.0 0.0 copy-start
  137.0 1.1 fusion.1
  138.1 0.1 concatenate.16
  138.2 0.1 concatenate.17
  138.2 1.0 pad_maximum_fusion
  139.3 0.0 copy-done
  139.3 0.8 copy.19
  (2 shorter events, 0.0 us)
Async XLA Ops:
  0.6 7.5 %copy-start.1 = (bf16[5120,32]{0,1:T(8,128)(2,1)S(1)}, bf16[5120,32]{0,1:T(8,128)(2,1)}, u32[]{:S(2)}) copy-start(bf16[5120,32]{0,1:T(8,128)(2,1)} %param.23) | copy-start | bytes 983044
  137.0 2.3 %copy-start = (bf16[64,4096]{1,0:T(8,128)(2,1)S(1)}, bf16[64,4096]{1,0:T(8,128)(2,1)}, u32[]{:S(2)}) copy-start(bf16[64,4096]{1,0:T(8,128)(2,1)} %get-tuple-element.15) | copy-start | bytes 1572868

commit v2 on v1

v2 whole, which is shorter than its diff:
```python
import math

import jax
import jax.numpy as jnp
from jax import lax
from jax.experimental import pallas as pl
from jax.experimental.pallas import tpu as pltpu
from jax.sharding import PartitionSpec as P

HEADS = 32
KV_HEADS = 8
HEAD_DIM = 128
STEPS = 2
EPSILON = 1e-06
ROPE_BASE = 1000000.0
MESH = pl.DeviceIdType.MESH
F32 = jnp.float32
BF16 = jnp.bfloat16
NEG = -1e30
C = math.log2(math.e) / math.sqrt(HEAD_DIM)
NT = (((1,), (1,)), ((), ()))
CHUNK = 1024
TILE = 256


def dot_nt(a, b):
    return lax.dot_general(a, b, NT, preferred_element_type=F32)


def kernel(
    q_ref, k_ref, v_ref, st_ref, gain_ref, cos_ref, sin_ref, len_ref,
    wq_ref, bq_ref, wk_ref, bk_ref, wv_ref, bv_ref, wo_ref,
    out_ref, dec_ref,
    kvbuf, qbuf, obuf, S, acc, mx, ls,
    wq_v, wk_v, wv_v, wo_v, dq_own, dq, kvp_own, kvp, pmsg, part, opart, rs0, slabs, rs, fbuf, fsib,
    SD, stv, q_v, k_v, v_v,
    in_sem, w_sem, kv0_recv, kv0_loc, kv0_send, q_recv, q_send, ag_recv, ag_send, sib_recv, sib_send,
    o_recv, o_send, dq_recv, dq_send, kvp_recv, kvp_send, part_recv, part_send,
    rs0_recv, rs0_send, rs_recv, rs_send, f_recv, f_send, fs_recv, fs_send,
):
    g = lax.axis_index("grp")
    t = lax.axis_index("tp")
    x, ylo = lax.rem(g, 4), lax.div(g, 4)
    yhi, z, core = lax.div(t, 16), lax.rem(lax.div(t, 2), 8), lax.rem(t, 2)
    y = yhi * 2 + ylo
    own = (ylo * 4 + x) * 2 + yhi

    def dev(xx, yy, zz, cc):
        return {"grp": lax.rem(yy, 2) * 4 + xx, "tp": lax.div(yy, 2) * 16 + zz * 2 + cc}

    def flip(bit, by):
        return bit + by * (1 - 2 * bit)

    def column(by):
        return x + by * (3 - 2 * x), y + by * (3 - 2 * y)

    def rcopy(src, dst, send, recv, to):
        return pltpu.make_async_remote_copy(
            src_ref=src, dst_ref=dst, send_sem=send, recv_sem=recv, device_id=to, device_id_type=MESH
        )

    def drain(ref, sem):
        pltpu.make_async_copy(ref, ref, sem).wait()

    def head_cols(ref, h, width=HEAD_DIM):
        return ref.at[:, pl.ds(pl.multiple_of(h * width, width), width)]

    half = wo_v.shape[1] // 2

    loads = [
        pltpu.make_async_copy(a, b, in_sem.at[i])
        for i, (a, b) in enumerate(((k_ref, k_v), (v_ref, v_v), (q_ref, q_v)))
    ]
    for c in loads:
        c.start()
    weights = [
        pltpu.make_async_copy(a, b, w_sem.at[i])
        for i, (a, b) in enumerate(((wq_ref, wq_v), (wk_ref, wk_v), (wv_ref, wv_v), (wo_ref, wo_v)))
    ]
    for w in weights:
        w.start()

    barrier = pltpu.get_barrier_semaphore()

    def greet(to):
        pl.semaphore_signal(barrier, inc=1, device_id=to, device_id_type=MESH)

    y2 = lax.rem(y + 2, 4)
    for dc in range(2):
        for dz in range(8):
            zz, cc = lax.rem(z + dz, 8), flip(core, dc)
            if dz or dc:
                greet(dev(x, y, zz, cc))
            greet(dev(3 - x, 3 - y, zz, cc))
            greet(dev(x, y2, zz, cc))
    for d in (1, 3):
        greet(dev(lax.rem(x + d, 4), y, z, core))
        greet(dev(x, lax.rem(y + d, 4), z, core))
    for c in loads:
        c.wait()
    pl.semaphore_wait(barrier, 51)

    for dz in (4, 3, 5, 2, 6, 1, 7):
        zz = lax.rem(z + dz, 8)
        for kv, ref in enumerate((k_v, v_v)):
            rcopy(
                head_cols(ref, zz), kvbuf.at[kv, own, z, core], kv0_send.at[kv], kv0_recv.at[kv],
                dev(x, y, zz, core),
            ).start()
    kv_local = [
        pltpu.make_async_copy(head_cols(ref, z), kvbuf.at[kv, own, z, core], kv0_loc.at[kv])
        for kv, ref in enumerate((k_v, v_v))
    ]
    for c in kv_local:
        c.start()
    def send_queries(dp):
        px, py = column(dp)
        for dz in (4, 3, 5, 2, 6, 1, 7, 0):
            zz = lax.rem(z + dz, 8)
            for dc in range(2):
                cc = flip(core, dc)
                src = head_cols(q_v, 4 * zz + 2 * flip(ylo, dp) + cc)
                dst = qbuf.at[ylo, z, core]
                if dz or dp or dc:
                    rcopy(src, dst, q_send.at[dp], q_recv.at[ylo], dev(px, py, zz, cc)).start()
                else:
                    pltpu.make_async_copy(src, dst, q_recv.at[ylo]).start()

    send_queries(0)

    def place(o1, o2):
        ox, oy = (1 - core) * o1 + core * o2, core * o1 + (1 - core) * o2
        return lax.rem(x + ox, 4), lax.rem(y + oy, 4)

    def chunk_of(o1, o2):
        xx, yy = place(o1, o2)
        return (lax.rem(yy, 2) * 4 + xx) * 2 + lax.div(yy, 2)

    def block(o1, o2, kv=None):
        return kvbuf.at[slice(None) if kv is None else kv, chunk_of(o1, o2), :, core]

    def toward(axis, step):
        xx, yy = place(step, 0) if axis == 1 else place(0, step)
        return dev(xx, yy, z, core)

    def send(src, sem, recv, to):
        rcopy(src, src, sem, recv, to).start()

    sibling = dev(x, y, z, 1 - core)

    def to_sibling(o1, o2):
        send(block(o1, o2), sib_send.at[o1, o2], sib_recv.at[o1, o2], sibling)

    def from_sibling(o1, o2):
        drain(kvbuf.at[:, chunk_of(o1, o2), :, 1 - core], sib_recv.at[o2, o1])

    def open_axis1():
        send(block(0, 0), ag_send.at[0, 0], ag_recv.at[3, 0, 0], toward(1, 1))
        send(block(0, 0), ag_send.at[0, 1], ag_recv.at[1, 0, 0], toward(1, 3))

    def open_axis2(o1):
        send(block(o1, 0), ag_send.at[1 + o1, 0], ag_recv.at[o1, 3, 0], toward(2, 1))
        send(block(o1, 0), ag_send.at[1 + o1, 1], ag_recv.at[o1, 1, 0], toward(2, 3))

    def pass_axis1():
        drain(block(3, 0), ag_recv.at[3, 0, 0])
        send(block(3, 0, 0), ag_send.at[0, 2], ag_recv.at[2, 0, 0], toward(1, 1))
        drain(block(1, 0), ag_recv.at[1, 0, 0])
        send(block(1, 0, 1), ag_send.at[0, 3], ag_recv.at[2, 0, 1], toward(1, 3))

    def pass_axis2(o1):
        drain(block(o1, 3), ag_recv.at[o1, 3, 0])
        send(block(o1, 3, 0), ag_send.at[1 + o1, 2], ag_recv.at[o1, 2, 0], toward(2, 1))
        drain(block(o1, 1), ag_recv.at[o1, 1, 0])
        send(block(o1, 1, 1), ag_send.at[1 + o1, 3], ag_recv.at[o1, 2, 1], toward(2, 3))
        to_sibling(o1, 3)
        to_sibling(o1, 1)

    def end_axis(o1, o2):
        for kv in range(2):
            drain(block(o1, o2, kv), ag_recv.at[o1, o2, kv])
        to_sibling(o1, o2)

    for kv in range(2):
        kv_local[kv].wait()
        drain(kvbuf.at[kv, own, pl.ds(0, 7), core], kv0_recv.at[kv])
    open_axis1()
    open_axis2(0)
    to_sibling(0, 0)
    send_queries(1)

    for s in range(16):
        stv[pl.ds(2 * s, 2), :] = st_ref[s].astype(F32)
    states = stv[...]
    scale = lax.rsqrt(jnp.mean(states * states, axis=1, keepdims=True) + EPSILON)
    normed = jnp.concatenate(
        [
            (states[:, j * 128 : (j + 1) * 128] * scale * gain_ref[j : j + 1, :].astype(F32)).astype(BF16)
            for j in range(states.shape[1] // 128)
        ],
        axis=1,
    )
    for w in weights:
        w.wait()
    odd = lax.rem(lax.broadcasted_iota(jnp.int32, (32, HEAD_DIM), 0), 2) == 1
    cosine = jnp.concatenate([cos_ref[...], cos_ref[...]], axis=1)
    sine = jnp.concatenate([-sin_ref[...], sin_ref[...]], axis=1)
    cosine = jnp.where(odd, cosine[1:2, :], cosine[0:1, :])
    sine = jnp.where(odd, sine[1:2, :], sine[0:1, :])

    def rotate(value):
        return value * cosine + pltpu.roll(value, HEAD_DIM // 2, 1) * sine

    query = jnp.dot(normed, wq_v[...], preferred_element_type=F32) + bq_ref[...].astype(F32)
    dq_own[...] = rotate(query).astype(BF16)
    quarter = lax.rem(t, 4)
    spread = (
        lax.broadcasted_iota(jnp.int32, (32, HEAD_DIM), 1)
        == lax.broadcasted_iota(jnp.int32, (32, HEAD_DIM), 0) + quarter * 32
    ).astype(F32)
    for i, (w, b) in enumerate(((wk_v, bk_ref), (wv_v, bv_ref))):
        narrow = dot_nt(normed, w[...]) + b[...].astype(F32)
        kvp_own[i] = jnp.dot(narrow, spread, precision=lax.Precision.HIGHEST, preferred_element_type=F32)

    def to_tp(target, src, dst, send, recv):
        @pl.when(target != t)
        def _():
            rcopy(src, dst, send, recv, {"grp": g, "tp": target}).start()

        @pl.when(target == t)
        def _():
            pltpu.make_async_copy(src, dst, recv).start()

    for i in range(4):
        target = (i // 2) * 16 + lax.div(t, 4) * 2 + i % 2
        to_tp(target, dq_own, dq.at[quarter], dq_send.at[i], dq_recv.at[quarter])
    for m in range(1, 4):
        target = lax.div(t, 4) * 4 + lax.rem(quarter + m, 4)
        rcopy(kvp_own, kvp.at[m - 1], kvp_send.at[m - 1], kvp_recv.at[m - 1], {"grp": g, "tp": target}).start()

    acc[...] = jnp.zeros_like(acc)
    mx[...] = jnp.full_like(mx, NEG)
    ls[...] = jnp.zeros_like(ls)
    low = own + ylo * (15 - 2 * own)

    def unit(slot, cc, diagonal):
        tiles = CHUNK // TILE
        keys = kvbuf[0, cc].reshape(CHUNK, HEAD_DIM)
        values = kvbuf[1, cc].reshape(CHUNK, HEAD_DIM)
        held = {}

        def scores(i):
            width = (i + 1) * TILE if diagonal else CHUNK
            rows = pl.ds(i * TILE, TILE)
            s = dot_nt(qbuf[slot, 2 * i : 2 * i + 2].reshape(TILE, HEAD_DIM), keys[:width])
            if diagonal:
                r = lax.broadcasted_iota(jnp.int32, (TILE, width), 0) + i * TILE
                s = jnp.where(lax.broadcasted_iota(jnp.int32, (TILE, width), 1) <= r, s, NEG)
            S[i % 2, :, :width] = s
            old = mx[slot, rows, :]
            new = jnp.maximum(old, jnp.max(s, axis=1, keepdims=True))
            mx[slot, rows, :] = new
            held[i] = (old, new)

        def mix(i):
            width = (i + 1) * TILE if diagonal else CHUNK
            rows = pl.ds(i * TILE, TILE)
            old, new = held.pop(i)
            p = jnp.exp2(S[i % 2, :, :width] * C - (new * C)[:, :1])
            shrink = jnp.exp2((old - new) * C)
            ls[slot, rows, :] = ls[slot, rows, :] * shrink + jnp.sum(p, axis=1, keepdims=True)
            gained = jnp.dot(p.astype(BF16), values[:width], preferred_element_type=F32)
            acc[slot, rows, :] = acc[slot, rows, :] * shrink + gained

        scores(0)
        for i in range(tiles):
            if i + 1 < tiles:
                scores(i + 1)
            mix(i)

    def send_output(slot):
        obuf[slot] = (acc[slot] / ls[slot]).astype(BF16).reshape(8, 2, 64, HEAD_DIM)
        dp = flip(slot, ylo)
        px, py = column(dp)
        for dz in range(8):
            zz = lax.rem(z + dz, 8)
            for dc in range(2):
                cc = flip(core, dc)
                src = obuf.at[slot, zz, cc]
                dst = head_cols(out_ref, 4 * z + 2 * ylo + core)

                def away(src=src, dst=dst, to=dev(px, py, zz, cc), dp=dp):
                    rcopy(src, dst, o_send.at[dp], o_recv, to).start()

                if dz or dc:
                    away()
                else:
                    pl.when(dp == 1)(away)

                    @pl.when(dp == 0)
                    def _():
                        pltpu.make_async_copy(src, dst, o_recv).start()

    def decode_attend():
        for i in range(4):
            drain(dq.at[i], dq_recv.at[i])
        limit = len_ref[0]
        yq = lax.rem(y + core, 4)
        queries = dq[...].reshape(128, HEAD_DIM)
        chunks = [(lax.rem(yq, 2) * 4 + i) * 2 + lax.div(yq, 2) for i in range(4)]
        top = jnp.full((128, 1), NEG, F32)
        for i, cc in enumerate(chunks):
            s = dot_nt(queries, kvbuf[0, cc].reshape(CHUNK, HEAD_DIM))
            allowed = lax.broadcasted_iota(jnp.int32, (128, CHUNK), 1) + cc * CHUNK < limit
            s = jnp.where(allowed, s, NEG)
            SD[i] = s
            top = jnp.maximum(top, jnp.max(s, axis=1, keepdims=True))
        total = jnp.zeros((128, 1), F32)
        mixed = jnp.zeros((128, HEAD_DIM), F32)
        for i, cc in enumerate(chunks):
            s = SD[i]
            p = jnp.where(s > 0.5 * NEG, jnp.exp2(s * C - top * C), 0.0)
            total = total + jnp.sum(p, axis=1, keepdims=True)
            mixed = mixed + jnp.dot(
                p.astype(BF16), kvbuf[1, cc].reshape(CHUNK, HEAD_DIM), preferred_element_type=F32
            )
        first = lax.broadcasted_iota(jnp.int32, (32, HEAD_DIM), 1) < 64
        for i in range(4):
            rows = slice(i * 32, i * 32 + 32)
            pmsg[i, 0] = mixed[rows]
            pmsg[i, 1] = jnp.where(first, top[rows], total[rows])
        for i in range(4):
            slot = yhi * 2 + core
            to_tp(4 * z + i, pmsg.at[i], part.at[slot], part_send.at[i], part_recv.at[slot])

    def decode_join():
        for i in range(4):
            drain(part.at[i], part_recv.at[i])
        for i in range(3):
            drain(kvp.at[i], kvp_recv.at[i])
        step_key = rotate(kvp_own[0] + kvp[0, 0] + kvp[1, 0] + kvp[2, 0]).astype(BF16).astype(F32)
        step_value = (kvp_own[1] + kvp[0, 1] + kvp[1, 1] + kvp[2, 1]).astype(BF16).astype(F32)
        step_query = dq_own[...].astype(F32)
        here = jnp.sum(step_query * step_key, axis=1, keepdims=True)
        before = jnp.sum(step_query * pltpu.roll(step_key, 1, 0), axis=1, keepdims=True)
        later = lax.rem(lax.broadcasted_iota(jnp.int32, (32, 1), 0), 2) == 1
        before = jnp.where(later, before, NEG)
        tops = [part[i, 1][:, :1] for i in range(4)]
        sums = [part[i, 1][:, 64:65] for i in range(4)]
        top = jnp.maximum(here, before)
        for m in tops:
            top = jnp.maximum(top, m)
        p_here = jnp.exp2((here - top) * C)
        p_before = jnp.where(later, jnp.exp2((before - top) * C), 0.0)
        total = p_here + p_before
        mixed = p_here.astype(BF16).astype(F32) * step_value
        mixed = mixed + p_before.astype(BF16).astype(F32) * pltpu.roll(step_value, 1, 0)
        for i in range(4):
            w = jnp.exp2((tops[i] - top) * C)
            total = total + w * sums[i]
            mixed = mixed + w * part[i, 0]
        attended = (mixed / total).astype(BF16)
        for i in range(2):
            opart[i] = jnp.dot(attended, wo_v[:, i * half : (i + 1) * half], preferred_element_type=F32)
        rcopy(opart.at[1 - core], rs0, rs0_send, rs0_recv, sibling).start()

    mine = yhi * 8 + z

    def decode_sum():
        drain(rs0, rs0_recv)
        both = opart[core] + rs0[...]
        for n in range(16):
            rows, first = slice(n // 4 * 8, n // 4 * 8 + 8), n % 4 * 640
            pieces = [both[rows, first + j * 128 : first + j * 128 + 128] for j in range(5)]
            slabs[n] = jnp.concatenate(pieces + pieces[:1], axis=0).astype(BF16)
        for n in range(16):
            zz, yy = lax.rem(z + n % 8, 8), flip(yhi, n // 8)
            src = slabs.at[yy * 8 + zz]
            if n:
                rcopy(src, rs.at[n], rs_send.at[n], rs_recv.at[n], dev(x, yy * 2 + ylo, zz, core)).start()
            else:
                pltpu.make_async_copy(src, rs.at[0], rs_recv.at[0]).start()

    def decode_spread():
        for n in range(16):
            drain(rs.at[n], rs_recv.at[n])
        total_rows = rs[0].astype(F32)
        for n in range(1, 16):
            total_rows = total_rows + rs[n].astype(F32)
        slabs[mine] = total_rows.astype(BF16)
        for n in range(16):
            zz, yy = lax.rem(z + n % 8, 8), flip(yhi, n // 8)
            if n:
                rcopy(slabs.at[mine], fbuf.at[mine], f_send.at[n], f_recv, dev(x, yy * 2 + ylo, zz, core)).start()
            else:
                pltpu.make_async_copy(slabs.at[mine], fbuf.at[mine], f_recv).start()

    def decode_swap():
        drain(fbuf, f_recv)
        rcopy(fbuf, fsib, fs_send, fs_recv, sibling).start()

    def decode_finish():
        drain(fsib, fs_recv)
        here = lax.broadcasted_iota(jnp.int32, fbuf.shape[1:], 0) * 0 + core == 0
        for part_no in range(2):
            for group in range(4):
                pieces = []
                for n in range(4 * group, 4 * group + 4):
                    a, b = (fbuf, fsib) if part_no == 0 else (fsib, fbuf)
                    block_rows = jnp.where(here, a[n].astype(F32), b[n].astype(F32))
                    pieces += [block_rows[8 * j : 8 * j + 8] for j in range(5)]
                rows = jnp.concatenate(pieces, axis=1).astype(BF16)
                for r in range(4):
                    dec_ref[4 * group + r, :, part_no * half : (part_no + 1) * half] = rows[2 * r : 2 * r + 2]

    order = (
        (0, 0), (1, 0), (0, 1), (3, 0), (0, 3), (2, 0), (0, 2), (1, 1), (1, 3),
        (3, 1), (3, 3), (1, 2), (2, 1), (3, 2), (2, 3), (2, 2),
    )
    early = 9

    def look_up(table, v):
        found = v * 0 + table[0]
        for n in range(1, len(table)):
            found = jnp.where(v == n, table[n], found)
        return found

    def place_of(v):
        return look_up([o[0] for o in order], v), look_up([o[1] for o in order], v)

    def hop1():
        pass_axis1()
        open_axis2(1)
        open_axis2(3)
        to_sibling(1, 0)
        to_sibling(3, 0)
        pass_axis2(0)

    def hop2():
        end_axis(2, 0)
        open_axis2(2)

    def hop3():
        pass_axis2(1)
        pass_axis2(3)

    def hop4():
        end_axis(0, 2)

    def hop5():
        pass_axis2(2)

    def hop6():
        end_axis(1, 2)
        end_axis(3, 2)
        end_axis(2, 2)

    def item(i):
        second = i >= 16 + early
        slot = jnp.where(i < 2 * early, lax.rem(i, 2), jnp.where(second, 1, 0))
        v = jnp.where(i < 2 * early, lax.div(i, 2), jnp.where(second, i - 16, i - early))
        o1, o2 = place_of(v)
        return slot, v, o1, o2, chunk_of(o1, o2), low + slot * (15 - 2 * low)

    hops = ((2, hop2), (3, hop3), (3, hop4), (4, hop5), (5, hop6))
    steps = (
        (7, decode_attend), (9, decode_join), (10, decode_sum), (13, decode_spread), (16, decode_swap),
    )

    def work(u, carry):
        at, level, seen = carry

        def skips(i):
            slot, v, o1, o2, cc, last = item(i)
            return cc > last

        now = lax.while_loop(skips, lambda i: i + 1, at)
        slot, v, o1, o2, cc, last = item(now)
        due = look_up((1, 2, 2, 3, 3, 4, 4, 5), jnp.minimum(u, 7))
        due = jnp.maximum(due, jnp.where(v <= 4, 1, jnp.where(v <= 10, 3, 5)))
        for needs, hop in hops:
            pl.when((level < needs) & (needs <= due))(hop)
        known = jnp.where(u == 7, 16, jnp.maximum(seen, v + 1))

        def learn(n, c):
            from_sibling(*place_of(n))
            return c

        lax.fori_loop(seen, known, learn, 0)
        pl.when((at <= 16 + early) & (now >= 16 + early))(lambda: send_output(0))
        for when, step in steps:
            pl.when(u == when)(step)

        @pl.when(cc < last)
        def _():
            unit(slot, cc, False)

        @pl.when(cc == last)
        def _():
            unit(slot, cc, True)

        return now + 1, jnp.maximum(level, due), known

    drain(qbuf.at[ylo], q_recv.at[ylo])

    def all_work(u, carry):
        @pl.when(u == 1)
        def _():
            hop1()
            drain(qbuf.at[1 - ylo], q_recv.at[1 - ylo])

        return work(u, carry)

    zero = t * 0
    lax.fori_loop(0, 17, all_work, (zero, zero + 1, zero))
    send_output(1)
    decode_finish()

    for n in range(1, 16):
        drain(rs.at[n], rs_send.at[n])
        drain(rs.at[n], f_send.at[n])
    for i in range(4):
        pl.when((i // 2) * 16 + lax.div(t, 4) * 2 + i % 2 != t)(lambda i=i: drain(dq_own, dq_send.at[i]))
        pl.when(4 * z + i != t)(lambda i=i: drain(pmsg.at[i], part_send.at[i]))
    for i in range(3):
        drain(kvp_own, kvp_send.at[i])
    for kv in range(2):
        drain(kvbuf.at[0, pl.ds(0, 7), 0, 0], kv0_send.at[kv])
    drain(kvbuf.at[0, pl.ds(0, 15), 0, 0], q_send.at[0])
    drain(kvbuf.at[0, pl.ds(0, 16), 0, 0], q_send.at[1])
    drain(kvbuf.at[0, pl.ds(0, 15), 0, 0], o_send.at[0])
    drain(kvbuf.at[0, pl.ds(0, 16), 0, 0], o_send.at[1])
    whole, half_block = kvbuf.at[:, 0, :, 0], kvbuf.at[0, 0, :, 0]
    for a in range(5):
        for b in range(4):
            drain(whole if b < 2 else half_block, ag_send.at[a, b])
    for o1 in range(4):
        for o2 in range(4):
            drain(whole, sib_send.at[o1, o2])
    drain(rs0, rs0_send)
    drain(fbuf, fs_send)
    drain(out_ref, o_recv)


def hand_over(a_ref, b_ref, out_ref, dec_ref):
    out_ref[...] = a_ref[...]
    dec_ref[...] = b_ref[...]


def shards(
    prompt_q, prompt_k, prompt_v, lengths, sample_states, norm_gain,
    w_query, b_query, w_key, b_key, w_value, b_value, w_out,
):
    samples, steps, width = sample_states.shape
    rows = samples * steps
    half_dim = HEAD_DIM // 2
    positions = (lengths[0] + jnp.arange(steps, dtype=jnp.int32)).astype(F32)[:, None]
    frequency = ROPE_BASE ** (-(2.0 * jnp.arange(half_dim, dtype=F32)) / HEAD_DIM)
    angles = positions * frequency
    cosine, sine = jnp.cos(angles), jnp.sin(angles)
    vmem = pl.BlockSpec(memory_space=pltpu.VMEM)
    smem = pl.BlockSpec(memory_space=pltpu.SMEM)
    hbm = pl.BlockSpec(memory_space=pl.ANY)
    dma = pltpu.SemaphoreType.DMA
    half = width // 2
    prefill, decoded = pl.pallas_call(
        kernel,
        out_shape=(
            jax.ShapeDtypeStruct(prompt_q.shape, BF16),
            jax.ShapeDtypeStruct(sample_states.shape, BF16),
        ),
        in_specs=[hbm, hbm, hbm, vmem, vmem, vmem, vmem, smem, hbm, vmem, hbm, vmem, hbm, vmem, hbm],
        out_specs=(vmem, vmem),
        scratch_shapes=[
            pltpu.VMEM((2, 16, 8, 2, 64, HEAD_DIM), BF16),
            pltpu.VMEM((2, 8, 2, 64, HEAD_DIM), BF16),
            pltpu.VMEM((2, 8, 2, 64, HEAD_DIM), BF16),
            pltpu.VMEM((2, TILE, CHUNK), F32),
            pltpu.VMEM((2, CHUNK, HEAD_DIM), F32),
            pltpu.VMEM((2, CHUNK, HEAD_DIM), F32),
            pltpu.VMEM((2, CHUNK, HEAD_DIM), F32),
            pltpu.VMEM(w_query.shape, BF16),
            pltpu.VMEM(w_key.shape[::-1], BF16),
            pltpu.VMEM(w_value.shape[::-1], BF16),
            pltpu.VMEM(w_out.shape, BF16),
            pltpu.VMEM((rows, HEAD_DIM), BF16),
            pltpu.VMEM((4, rows, HEAD_DIM), BF16),
            pltpu.VMEM((2, rows, HEAD_DIM), F32),
            pltpu.VMEM((3, 2, rows, HEAD_DIM), F32),
            pltpu.VMEM((4, 2, rows, HEAD_DIM), F32),
            pltpu.VMEM((4, 2, rows, HEAD_DIM), F32),
            pltpu.VMEM((2, rows, half), F32),
            pltpu.VMEM((rows, half), F32),
            pltpu.VMEM((16, 48, HEAD_DIM), BF16),
            pltpu.VMEM((16, 48, HEAD_DIM), BF16),
            pltpu.VMEM((16, 48, HEAD_DIM), BF16),
            pltpu.VMEM((16, 48, HEAD_DIM), BF16),
            pltpu.VMEM((4, 4 * rows, CHUNK), F32),
            pltpu.VMEM((rows, width), F32),
            pltpu.VMEM(prompt_q.shape, BF16),
            pltpu.VMEM(prompt_k.shape, BF16),
            pltpu.VMEM(prompt_v.shape, BF16),
            dma((3,)),
            dma((4,)),
            dma((2,)), dma((2,)), dma((2,)),
            dma((2,)), dma((2,)),
            dma((4, 4, 2)), dma((5, 4)), dma((4, 4)), dma((4, 4)),
            dma, dma((2,)),
            dma((4,)), dma((4,)),
            dma((3,)), dma((3,)),
            dma((4,)), dma((4,)),
            dma, dma, dma((16,)), dma((16,)), dma, dma((16,)), dma, dma,
        ],
        compiler_params=pltpu.CompilerParams(
            collective_id=0, has_side_effects=True, vmem_limit_bytes=56 * 2**20
        ),
    )(
        prompt_q, prompt_k, prompt_v, sample_states, norm_gain.reshape(-1, 128),
        cosine, sine, lengths, w_query, b_query[None], w_key.T, b_key[None],
        w_value.T, b_value[None], w_out,
    )
    return pl.pallas_call(
        hand_over,
        out_shape=(
            jax.ShapeDtypeStruct(prefill.shape, BF16),
            jax.ShapeDtypeStruct(decoded.shape, BF16),
        ),
        in_specs=[vmem, vmem],
        out_specs=(vmem, vmem),
    )(prefill, decoded)


def solution(mesh):
    in_specs = (
        P(("grp", "tp"), None),
        P(("grp", "tp"), None),
        P(("grp", "tp"), None),
        P("grp"),
        P("grp", None, None),
        P(),
        P(None, "tp"),
        P("tp"),
        P(None, "tp"),
        P("tp"),
        P(None, "tp"),
        P("tp"),
        P("tp", None),
    )
    out_specs = (P(("grp", "tp"), None), P("grp", None, None))
    return jax.shard_map(shards, mesh=mesh, in_specs=in_specs, out_specs=out_specs, check_vma=False)
```

time: 141 us -> 105 us (0.74)
  Pallas kernels: 127 us -> 102 us
  local copies, waits for them, and re-layouts: 9.98 us -> 0 us
    pallas_call x1, Pallas kernels: 127 us -> 99.6 us  [shards(): pl.pallas_call(kernel, out_shape=(jax.ShapeDtypeStruct(prompt_q.shape, BF...]
    unnamed x7 -> x0, local copies, waits for them, and re-layouts: 4.42 us -> none
    pallas_call x0 -> x1, Pallas kernels: none -> 2.06 us  [shards(): pl.pallas_call(hand_over, out_shape=(jax.ShapeDtypeStruct(prefill.shape,...]
    reshape x1 -> x0, local copies, waits for them, and re-layouts: 1.82 us -> none  [shards(): sample_states.reshape(rows, width)]
where the time goes in v2:
time: 105 us; the launch traced here: 104 us
  Pallas kernels  102 us (97%)
  between operations  1.3 us (1%)
    pallas_call x1, Pallas kernels, shards(): pl.pallas_call(kernel, out_shape=(jax.ShapeDtypeStruct(prompt_q.shape, BF...  99.6 us

profile of v2, /device:TPU:25, one launch (start us, length us, event | category | flops | bytes accessed | tf_op | source)
XLA Modules:
  0.0 103.6 jit_solution(4815244094443591054)
XLA Ops:
  1.3 0.7 multiply_sine_fusion
  2.0 99.6 %shard_map.140 = (bf16[64,4096]{1,0:T(8,128)(2,1)}, bf16[16,2,5120]{2,1,0:T(2,128)(2,1)}) custom-call(bf16[64,4096]{1,0:T(8,128)(2,1)} %q_ref.1, bf16[64,1024]{1,0:T(8,128)(2,1)} %k_ref.1, bf16[64,1024]{1,0:T(8,128)(2,1)} %v_ref.1, bf16[16,2,5120]{2,1,0:T(2,128)(2,1)} %st_ref.1, bf16[40,128]{1,0:T(8,128)(2,1)} %bitcast.10, ...), custom_call_target="tpu_custom_call" | custom-call | tf_op jit(solution)/shard_map/pallas_call | solution.py:566
  101.6 2.1 %shard_map.141 = (bf16[64,4096]{1,0:T(8,128)(2,1)}, bf16[16,2,5120]{2,1,0:T(2,128)(2,1)}) custom-call(bf16[64,4096]{1,0:T(8,128)(2,1)} %get-tuple-element.4.a_ref, bf16[16,2,5120]{2,1,0:T(2,128)(2,1)} %get-tuple-element.5.b_ref), custom_call_target="tpu_custom_call" | custom-call | tf_op jit(solution)/shard_map/pallas_call | solution.py:622
  (2 shorter events, 0.0 us)

commit v3 on v2

--- a/solution.py
+++ b/solution.py
@@ -128,67 +128,6 @@
 
     send_queries(0)
 
-    def place(o1, o2):
-        ox, oy = (1 - core) * o1 + core * o2, core * o1 + (1 - core) * o2
-        return lax.rem(x + ox, 4), lax.rem(y + oy, 4)
-
-    def chunk_of(o1, o2):
-        xx, yy = place(o1, o2)
-        return (lax.rem(yy, 2) * 4 + xx) * 2 + lax.div(yy, 2)
-
-    def block(o1, o2, kv=None):
-        return kvbuf.at[slice(None) if kv is None else kv, chunk_of(o1, o2), :, core]
-
-    def toward(axis, step):
-        xx, yy = place(step, 0) if axis == 1 else place(0, step)
-        return dev(xx, yy, z, core)
-
-    def send(src, sem, recv, to):
-        rcopy(src, src, sem, recv, to).start()
-
-    sibling = dev(x, y, z, 1 - core)
-
-    def to_sibling(o1, o2):
-        send(block(o1, o2), sib_send.at[o1, o2], sib_recv.at[o1, o2], sibling)
-
-    def from_sibling(o1, o2):
-        drain(kvbuf.at[:, chunk_of(o1, o2), :, 1 - core], sib_recv.at[o2, o1])
-
-    def open_axis1():
-        send(block(0, 0), ag_send.at[0, 0], ag_recv.at[3, 0, 0], toward(1, 1))
-        send(block(0, 0), ag_send.at[0, 1], ag_recv.at[1, 0, 0], toward(1, 3))
-
-    def open_axis2(o1):
-        send(block(o1, 0), ag_send.at[1 + o1, 0], ag_recv.at[o1, 3, 0], toward(2, 1))
-        send(block(o1, 0), ag_send.at[1 + o1, 1], ag_recv.at[o1, 1, 0], toward(2, 3))
-
-    def pass_axis1():
-        drain(block(3, 0), ag_recv.at[3, 0, 0])
-        send(block(3, 0, 0), ag_send.at[0, 2], ag_recv.at[2, 0, 0], toward(1, 1))
-        drain(block(1, 0), ag_recv.at[1, 0, 0])
-        send(block(1, 0, 1), ag_send.at[0, 3], ag_recv.at[2, 0, 1], toward(1, 3))
-
-    def pass_axis2(o1):
-        drain(block(o1, 3), ag_recv.at[o1, 3, 0])
-        send(block(o1, 3, 0), ag_send.at[1 + o1, 2], ag_recv.at[o1, 2, 0], toward(2, 1))
-        drain(block(o1, 1), ag_recv.at[o1, 1, 0])
-        send(block(o1, 1, 1), ag_send.at[1 + o1, 3], ag_recv.at[o1, 2, 1], toward(2, 3))
-        to_sibling(o1, 3)
-        to_sibling(o1, 1)
-
-    def end_axis(o1, o2):
-        for kv in range(2):
-            drain(block(o1, o2, kv), ag_recv.at[o1, o2, kv])
-        to_sibling(o1, o2)
-
-    for kv in range(2):
-        kv_local[kv].wait()
-        drain(kvbuf.at[kv, own, pl.ds(0, 7), core], kv0_recv.at[kv])
-    open_axis1()
-    open_axis2(0)
-    to_sibling(0, 0)
-    send_queries(1)
-
     for s in range(16):
         stv[pl.ds(2 * s, 2), :] = st_ref[s].astype(F32)
     states = stv[...]
@@ -241,6 +180,68 @@
     acc[...] = jnp.zeros_like(acc)
     mx[...] = jnp.full_like(mx, NEG)
     ls[...] = jnp.zeros_like(ls)
+
+    def place(o1, o2):
+        ox, oy = (1 - core) * o1 + core * o2, core * o1 + (1 - core) * o2
+        return lax.rem(x + ox, 4), lax.rem(y + oy, 4)
+
+    def chunk_of(o1, o2):
+        xx, yy = place(o1, o2)
+        return (lax.rem(yy, 2) * 4 + xx) * 2 + lax.div(yy, 2)
+
+    def block(o1, o2, kv=None):
+        return kvbuf.at[slice(None) if kv is None else kv, chunk_of(o1, o2), :, core]
+
+    def toward(axis, step):
+        xx, yy = place(step, 0) if axis == 1 else place(0, step)
+        return dev(xx, yy, z, core)
+
+    def send(src, sem, recv, to):
+        rcopy(src, src, sem, recv, to).start()
+
+    sibling = dev(x, y, z, 1 - core)
+
+    def to_sibling(o1, o2):
+        send(block(o1, o2), sib_send.at[o1, o2], sib_recv.at[o1, o2], sibling)
+
+    def from_sibling(o1, o2):
+        drain(kvbuf.at[:, chunk_of(o1, o2), :, 1 - core], sib_recv.at[o2, o1])
+
+    def open_axis1():
+        send(block(0, 0), ag_send.at[0, 0], ag_recv.at[3, 0, 0], toward(1, 1))
+        send(block(0, 0), ag_send.at[0, 1], ag_recv.at[1, 0, 0], toward(1, 3))
+
+    def open_axis2(o1):
+        send(block(o1, 0), ag_send.at[1 + o1, 0], ag_recv.at[o1, 3, 0], toward(2, 1))
+        send(block(o1, 0), ag_send.at[1 + o1, 1], ag_recv.at[o1, 1, 0], toward(2, 3))
+
+    def pass_axis1():
+        drain(block(3, 0), ag_recv.at[3, 0, 0])
+        send(block(3, 0, 0), ag_send.at[0, 2], ag_recv.at[2, 0, 0], toward(1, 1))
+        drain(block(1, 0), ag_recv.at[1, 0, 0])
+        send(block(1, 0, 1), ag_send.at[0, 3], ag_recv.at[2, 0, 1], toward(1, 3))
+
+    def pass_axis2(o1):
+        drain(block(o1, 3), ag_recv.at[o1, 3, 0])
+        send(block(o1, 3, 0), ag_send.at[1 + o1, 2], ag_recv.at[o1, 2, 0], toward(2, 1))
+        drain(block(o1, 1), ag_recv.at[o1, 1, 0])
+        send(block(o1, 1, 1), ag_send.at[1 + o1, 3], ag_recv.at[o1, 2, 1], toward(2, 3))
+        to_sibling(o1, 3)
+        to_sibling(o1, 1)
+
+    def end_axis(o1, o2):
+        for kv in range(2):
+            drain(block(o1, o2, kv), ag_recv.at[o1, o2, kv])
+        to_sibling(o1, o2)
+
+    for kv in range(2):
+        kv_local[kv].wait()
+        drain(kvbuf.at[kv, own, pl.ds(0, 7), core], kv0_recv.at[kv])
+    open_axis1()
+    open_axis2(0)
+    to_sibling(0, 0)
+    send_queries(1)
+
     low = own + ylo * (15 - 2 * own)
 
     def unit(slot, cc, diagonal):
@@ -464,7 +465,7 @@
 
     hops = ((2, hop2), (3, hop3), (3, hop4), (4, hop5), (5, hop6))
     steps = (
-        (7, decode_attend), (9, decode_join), (10, decode_sum), (13, decode_spread), (16, decode_swap),
+        (6, decode_attend), (8, decode_join), (9, decode_sum), (12, decode_spread), (16, decode_swap),
     )
 
     def work(u, carry):
@@ -476,11 +477,11 @@
 
         now = lax.while_loop(skips, lambda i: i + 1, at)
         slot, v, o1, o2, cc, last = item(now)
-        due = look_up((1, 2, 2, 3, 3, 4, 4, 5), jnp.minimum(u, 7))
+        due = look_up((1, 2, 2, 3, 3, 4, 5), jnp.minimum(u, 6))
         due = jnp.maximum(due, jnp.where(v <= 4, 1, jnp.where(v <= 10, 3, 5)))
         for needs, hop in hops:
             pl.when((level < needs) & (needs <= due))(hop)
-        known = jnp.where(u == 7, 16, jnp.maximum(seen, v + 1))
+        known = jnp.where(u == 6, 16, jnp.maximum(seen, v + 1))
 
         def learn(n, c):
             from_sibling(*place_of(n))

time: 105 us -> 102 us (0.971)
  Pallas kernels: 102 us -> 98.4 us
    pallas_call x1, Pallas kernels: 99.6 us -> 96.3 us  [shards(): pl.pallas_call(kernel, out_shape=(jax.ShapeDtypeStruct(prompt_q.shape, BF...]
where the time goes in v3:
time: 102 us; the launch traced here: 100 us
  Pallas kernels  98.4 us (96%)
  between operations  1.3 us (1%)
    pallas_call x1, Pallas kernels, shards(): pl.pallas_call(kernel, out_shape=(jax.ShapeDtypeStruct(prompt_q.shape, BF...  96.3 us
    pallas_call x1, Pallas kernels, shards(): pl.pallas_call(hand_over, out_shape=(jax.ShapeDtypeStruct(prefill.shape,...  2.06 us

profile of v3, /device:TPU:25, one launch (start us, length us, event | category | flops | bytes accessed | tf_op | source)
XLA Modules:
  0.0 100.4 jit_solution(17250356856599406987)
XLA Ops:
  1.3 0.7 multiply_sine_fusion
  2.0 96.3 %shard_map.140 = (bf16[64,4096]{1,0:T(8,128)(2,1)}, bf16[16,2,5120]{2,1,0:T(2,128)(2,1)}) custom-call(bf16[64,4096]{1,0:T(8,128)(2,1)} %q_ref.1, bf16[64,1024]{1,0:T(8,128)(2,1)} %k_ref.1, bf16[64,1024]{1,0:T(8,128)(2,1)} %v_ref.1, bf16[16,2,5120]{2,1,0:T(2,128)(2,1)} %st_ref.1, bf16[40,128]{1,0:T(8,128)(2,1)} %bitcast.10, ...), custom_call_target="tpu_custom_call" | custom-call | tf_op jit(solution)/shard_map/pallas_call | solution.py:567
  98.3 2.1 %shard_map.141 = (bf16[64,4096]{1,0:T(8,128)(2,1)}, bf16[16,2,5120]{2,1,0:T(2,128)(2,1)}) custom-call(bf16[64,4096]{1,0:T(8,128)(2,1)} %get-tuple-element.4.a_ref, bf16[16,2,5120]{2,1,0:T(2,128)(2,1)} %get-tuple-element.5.b_ref), custom_call_target="tpu_custom_call" | custom-call | tf_op jit(solution)/shard_map/pallas_call | solution.py:623
  (2 shorter events, 0.0 us)

commit v4 on v3

--- a/solution.py
+++ b/solution.py
@@ -465,7 +465,7 @@
 
     hops = ((2, hop2), (3, hop3), (3, hop4), (4, hop5), (5, hop6))
     steps = (
-        (6, decode_attend), (8, decode_join), (9, decode_sum), (12, decode_spread), (16, decode_swap),
+        (6, decode_attend), (8, decode_join), (9, decode_sum), (13, decode_spread),
     )
 
     def work(u, carry):
@@ -515,6 +515,7 @@
     zero = t * 0
     lax.fori_loop(0, 17, all_work, (zero, zero + 1, zero))
     send_output(1)
+    decode_swap()
     decode_finish()
 
     for n in range(1, 16):

time: 102 us -> 100 us (0.980); the launches traced: 100 us -> 100 us
  no operation moved by 1% of the time
where the time goes in v4:
time: 100 us
  Pallas kernels  98.1 us (98%)
  between operations  1.3 us (1%)
    pallas_call x1, Pallas kernels, shards(): pl.pallas_call(kernel, out_shape=(jax.ShapeDtypeStruct(prompt_q.shape, BF...  96.1 us
    pallas_call x1, Pallas kernels, shards(): pl.pallas_call(hand_over, out_shape=(jax.ShapeDtypeStruct(prefill.shape,...  2.06 us

profile of v4, /device:TPU:25, one launch (start us, length us, event | category | flops | bytes accessed | tf_op | source)
XLA Modules:
  0.0 100.1 jit_solution(6068621511783829050)
XLA Ops:
  1.3 0.7 multiply_sine_fusion
  2.0 96.1 %shard_map.140 = (bf16[64,4096]{1,0:T(8,128)(2,1)}, bf16[16,2,5120]{2,1,0:T(2,128)(2,1)}) custom-call(bf16[64,4096]{1,0:T(8,128)(2,1)} %q_ref.1, bf16[64,1024]{1,0:T(8,128)(2,1)} %k_ref.1, bf16[64,1024]{1,0:T(8,128)(2,1)} %v_ref.1, bf16[16,2,5120]{2,1,0:T(2,128)(2,1)} %st_ref.1, bf16[40,128]{1,0:T(8,128)(2,1)} %bitcast.10, ...), custom_call_target="tpu_custom_call" | custom-call | tf_op jit(solution)/shard_map/pallas_call | solution.py:568
  98.1 2.1 %shard_map.141 = (bf16[64,4096]{1,0:T(8,128)(2,1)}, bf16[16,2,5120]{2,1,0:T(2,128)(2,1)}) custom-call(bf16[64,4096]{1,0:T(8,128)(2,1)} %get-tuple-element.4.a_ref, bf16[16,2,5120]{2,1,0:T(2,128)(2,1)} %get-tuple-element.5.b_ref), custom_call_target="tpu_custom_call" | custom-call | tf_op jit(solution)/shard_map/pallas_call | solution.py:624
  (2 shorter events, 0.0 us)
